TPU v7x, 256 devices: a whole 4x4x8 slice. The times are simulated.
256 devices in a mesh: section: 16 (over y_lo, z), ctx: 16 (over y_hi, x, core).
Axes of the slice: x: 4, y: 4 (y_hi: 2, y_lo: 2; y = y_hi * 2 + y_lo), z: 8, core: 2. Of those that a mesh axis runs over, the one named last changes fastest.
Arguments:
- layer_input: bfloat16 [16, 4096, 2048], P('section', 'ctx'), may hold values from -6 to 6
- qk_weight: bfloat16 [16, 2048, 2048], P('section'), may hold values from -0.125 to 0.125
- norm_gain: float32 [16, 2048], P('section'), may hold values from 0.25 to 1.75
- out_gain: float32 [16, 128], P('section'), may hold values from 0.25 to 1.75
- log_decay: float32 [16, 16, 4096], P('section', None, 'ctx'), may hold values from -1 to 0
- write_rate: float32 [16, 16, 4096], P('section', None, 'ctx'), may hold values from 0 to 1
Outputs:
- layer_output: bfloat16 [16, 4096, 2048], P('section', 'ctx')
All inputs are finite; a program needn't handle non-finite values.
Results may differ from a plain program's by a relative error of at most 0.015.
Values may be sent and summed in bfloat16 or wider, within the bound.
No kernel may reach another device: no remote copies, remote signals or barrier semaphores. Data moves between devices by JAX's collectives and lax.ppermute only.
A program may use at most 192 MiB of HBM per device.

v0:
```python
import functools

import jax
import jax.numpy as jnp
from jax import lax
from jax.experimental import pallas as pl
from jax.experimental.pallas import tpu as pltpu
from jax.sharding import PartitionSpec as P

F32 = jnp.float32
BF16 = jnp.bfloat16
EPS = 1e-6
HALF = 128
BASE = 8
GROUP = 8
XS = 4
VMEM = pl.BlockSpec(memory_space=pltpu.VMEM)


def in_hbm(array):
    return pltpu.with_memory_space_constraint(array, pltpu.HBM)


def place():
    at = lax.axis_index("ctx")
    return at % 2, at // 2 % XS


def mm(a, b):
    return jnp.dot(a, b, preferred_element_type=F32)


def iota(shape, dim):
    return lax.broadcasted_iota(jnp.int32, shape, dim)


def base_inverses(couplings):
    lanes = HALF
    count = len(couplings)
    blocks = lanes // BASE
    lane = iota((BASE, lanes), 1)
    packed = []
    for c in couplings:
        d = jnp.zeros((BASE, lanes), F32)
        for blk in range(blocks):
            d = jnp.where(lane // BASE == blk, c[blk * BASE : (blk + 1) * BASE, :], d)
        packed.append(d)
    d = jnp.concatenate(packed, axis=0)
    rows = count * BASE
    lane_all = iota((rows, lanes), 1)
    x = jnp.where(iota((rows, lanes), 0) % BASE == lane_all % BASE, 1.0, 0.0).astype(F32)
    x = x.reshape(count, BASE, lanes)
    for j in range(BASE - 1):
        spread = jnp.take_along_axis(d, lane_all // BASE * BASE + j, axis=1)
        x = x - spread.reshape(count, BASE, lanes) * x[:, j : j + 1, :]
    full = []
    for n in range(count):
        full.append(
            jnp.concatenate(
                [jnp.where(lane // BASE == blk, x[n], 0.0) for blk in range(blocks)], axis=0
            )
        )
    return full


def merge(inverses, couplings, m):
    kind = F32 if m < 16 else BF16
    size = HALF
    pairs = size // (2 * m)
    lane = iota((m, size), 1)
    odd_at = [(2 * p + 1) * m for p in range(pairs)]
    couplings = [c.astype(kind) for c in couplings]
    left = [
        jnp.concatenate(
            [
                jnp.where(lane // m == 2 * p, c[at : at + m, :], jnp.zeros((), kind))
                for p, at in enumerate(odd_at)
            ],
            axis=0,
        ).astype(BF16)
        for c in couplings
    ]
    middle = [mm(a, x.astype(BF16)).astype(kind) for a, x in zip(left, inverses)]
    blank = jnp.zeros((m, size), kind)
    spread = [
        jnp.concatenate(
            [part for p in range(pairs) for part in (blank, y[p * m : (p + 1) * m, :])], axis=0
        ).astype(BF16)
        for y in middle
    ]
    odd = [jnp.concatenate([x[at : at + m, :] for at in odd_at], axis=0) for x in inverses]
    lower = [mm(a.astype(BF16), y).astype(kind) for a, y in zip(odd, spread)]
    return [
        jnp.concatenate(
            [
                part
                for p, at in enumerate(odd_at)
                for part in (x[at - m : at, :], (o - z)[p * m : (p + 1) * m, :])
            ],
            axis=0,
        ).astype(BF16)
        for x, o, z in zip(inverses, odd, lower)
    ]


def split3(value):
    hi = value.astype(BF16)
    rest = value - hi.astype(F32)
    mid = rest.astype(BF16)
    return hi, mid, (rest - mid.astype(F32)).astype(BF16)


def fetch(pairs, sems):
    copies = [pltpu.make_async_copy(a, b, sems.at[n]) for n, (a, b) in enumerate(pairs)]
    for copy in copies:
        copy.start()
    return copies


def decays(n, cumul, cols):
    tokens = cols.shape[0]
    half = HALF
    incl = iota((half, half), 1) <= iota((half, half), 0)
    c = jnp.broadcast_to(cols[:, n : n + 1], (tokens, half))
    c_row = cumul[n : n + 1, :]
    c_mid = c_row[:, half - 1 : half]
    d00 = jnp.where(incl, jnp.exp(c[:half] - c_row[:, :half]), 0.0)
    d11 = jnp.where(incl, jnp.exp(c[half:] - c_row[:, half:]), 0.0)
    d10 = jnp.exp(c[half:] - c_mid) * jnp.exp(c_mid - c_row[:, :half])
    return c, c_row, d00, d10, d11


def group_pairs(s, normed, weight, cumul, cols, pairs_ref, unit_keys, solved_ref):
    tokens, width = normed.shape
    heads_all = cumul.shape[0]
    half = HALF
    core, _ = place()
    ri = iota((half, half), 0)
    ci = iota((half, half), 1)
    strict = ci < ri
    eye = ri == ci
    pk = mm(normed[...], weight)
    heads = []
    for h in range(GROUP):
        n = s * GROUP + h
        if h % 2 == 0:
            at = h // 2 * 128
            raw = pk[:, at : at + 128]
            k = (raw * lax.rsqrt(jnp.sum(raw * raw, axis=-1, keepdims=True) + EPS)).astype(BF16)
            unit_keys[:, at : at + 128] = k
            kt = k.T
            g0 = mm(k[:half], kt[:, :half])
            g1 = mm(k[half:], kt)
            kf = k.astype(F32)
            ktf = kt.astype(F32)
        c, c_row, d00, d10, d11 = decays(n, cumul, cols)
        b = jnp.broadcast_to(cols[:, heads_all + n : heads_all + n + 1], (tokens, half))
        c_end = c_row[:, tokens - 1 : tokens]
        l00 = jnp.where(strict, b[:half] * d00 * g0, 0.0)
        l11 = jnp.where(strict, b[half:] * d11 * g1[:, half:], 0.0)
        l10 = (b[half:] * d10 * g1[:, :half]).astype(BF16)
        v_at = pl.multiple_of((n * 128 + (1 - core) * (width // 2)) % width, 128)
        v = normed[:, pl.ds(v_at, 128)].astype(F32)
        right = jnp.concatenate([(b * v).astype(BF16), (b * jnp.exp(c) * kf).astype(BF16)], axis=1)
        carried_t = (ktf * jnp.exp(c_end - c_row)).astype(BF16)
        heads.append((l00, l11, l10, right, carried_t, jnp.exp(c_end)))

    inverses = base_inverses([c for hd in heads for c in hd[:2]])
    couplings = [c for hd in heads for c in hd[:2]]
    m = BASE
    while m < half:
        inverses = merge(inverses, couplings, m)
        m *= 2

    tops = [mm(x, hd[3][:half]).astype(BF16) for x, hd in zip(inverses[::2], heads)]
    rests = [
        (hd[3][half:].astype(F32) - mm(hd[2], top)).astype(BF16) for hd, top in zip(heads, tops)
    ]
    lows = [mm(x, rest).astype(BF16) for x, rest in zip(inverses[1::2], rests)]
    for h in range(GROUP):
        solved = jnp.concatenate([tops[h], lows[h]], axis=0)
        solved_ref[h] = solved
        pair = mm(heads[h][4], solved)
        pairs_ref[h, 0] = (jnp.where(eye, heads[h][5], 0.0) - pair[:, 128:]).astype(BF16)
        pairs_ref[h, 1] = pair[:, :128].astype(BF16)


def first_kernel(
    x_hbm, gain_hbm, decay_hbm, rate_hbm, w_hbm,
    pairs_ref, unit_keys, solved_ref, xbuf, normed, wk, wq, cumul_ref, cols_ref,
    gains, logs_buf, rates_buf, sems,
):
    tokens, width = xbuf.shape
    steps = wk.shape[0]
    wcols = wk.shape[2]
    heads_all = logs_buf.shape[0]
    mid_head = heads_all // 2
    core, _ = place()
    here = pl.multiple_of(core * mid_head, mid_head)
    there = pl.multiple_of((1 - core) * mid_head, mid_head)
    pairs = [(x_hbm, xbuf), (gain_hbm, gains)]
    for at, frm in ((0, there), (mid_head, here)):
        pairs.append((decay_hbm.at[pl.ds(frm, mid_head)], logs_buf.at[pl.ds(at, mid_head)]))
        pairs.append((rate_hbm.at[pl.ds(frm, mid_head)], rates_buf.at[pl.ds(at, mid_head)]))
    w_at = len(pairs)
    for base, to in ((width // 2, wk), (0, wq)):
        for s in range(steps):
            frm = (s * wcols + (1 - core) * (width // 4)) % (width // 2)
            frm = pl.multiple_of(base + frm, 128)
            pairs.append((w_hbm.at[:, pl.ds(frm, wcols)], to.at[s]))
    copies = fetch(pairs, sems)

    for copy in copies[2:w_at]:
        copy.wait()
    upto = (iota((tokens, tokens), 0) <= iota((tokens, tokens), 1)).astype(BF16)
    hi, mid, low = split3(logs_buf[...])
    cumul = mm(hi, upto) + (mm(mid, upto) + mm(low, upto))
    cols = jnp.concatenate([cumul, rates_buf[...]], axis=0).T
    cumul_ref[...] = cumul
    cols_ref[...] = cols

    copies[0].wait()
    copies[1].wait()
    for r in range(0, tokens, 64):
        xf = xbuf[r : r + 64, :].astype(F32)
        normed[r : r + 64, :] = (
            xf * lax.rsqrt(jnp.mean(xf * xf, axis=-1, keepdims=True) + EPS) * gains[...]
        ).astype(BF16)

    copies[w_at].wait()
    group_pairs(0, normed, wk[0], cumul, cols, pairs_ref, unit_keys, solved_ref)
    for copy in copies[w_at + 1 :]:
        copy.wait()


def last_kernel(normed, wk, cumul_ref, cols_ref, pairs_ref, unit_keys, solved_ref):
    group_pairs(
        1, normed, wk[1], cumul_ref[...], cols_ref[...], pairs_ref, unit_keys, solved_ref
    )


def group_shapes(x, heads):
    tokens, width = x.shape
    return [
        jax.ShapeDtypeStruct((GROUP, 2, 128, 128), BF16),
        jax.ShapeDtypeStruct((tokens, GROUP // 2 * 128), BF16),
        jax.ShapeDtypeStruct((GROUP, tokens, 256), BF16),
    ]


def pairs_call(kernel, in_specs, outs, scratch, name, args):
    return pl.pallas_call(
        kernel,
        in_specs=in_specs,
        out_specs=[VMEM] * len(outs),
        out_shape=outs,
        scratch_shapes=scratch,
        compiler_params=pltpu.CompilerParams(vmem_limit_bytes=24 * 1024 * 1024),
        cost_estimate=pl.CostEstimate(
            flops=5_000_000_000, bytes_accessed=8_000_000, transcendentals=1_000_000
        ),
        name=name,
    )(*args)


def first_pairs(x, weight, gain_in, log_decay, write_rate):
    tokens, width = x.shape
    heads = log_decay.shape[0]
    steps = heads // GROUP
    wcols = GROUP // 2 * 128
    weights = jax.ShapeDtypeStruct((steps, width, wcols), BF16)
    return pairs_call(
        first_kernel,
        [pl.BlockSpec(memory_space=pltpu.HBM)] * 5,
        group_shapes(x, heads)
        + [
            jax.ShapeDtypeStruct((tokens, width), BF16),
            jax.ShapeDtypeStruct((tokens, width), BF16),
            weights,
            weights,
            jax.ShapeDtypeStruct((heads, tokens), F32),
            jax.ShapeDtypeStruct((tokens, 2 * heads), F32),
        ],
        [
            pltpu.VMEM((1, width), F32),
            pltpu.VMEM((heads, tokens), F32),
            pltpu.VMEM((heads, tokens), F32),
            pltpu.SemaphoreType.DMA((6 + 2 * steps,)),
        ],
        "first_pairs",
        [in_hbm(a) for a in (x, gain_in, log_decay, write_rate, weight)],
    )


def last_pairs(normed, wk, cumul, cols):
    return pairs_call(
        last_kernel,
        [VMEM] * 4,
        group_shapes(normed, cumul.shape[0]),
        [],
        "last_pairs",
        (normed, wk, cumul, cols),
    )


def rows_kernel(s, normed, wq, unit_keys, solved_ref, cumul_ref, cols_ref, rows_ref):
    half = HALF
    tokens = normed.shape[0]
    pq = mm(normed[...], wq[s])
    cumul = cumul_ref[...]
    cols = cols_ref[...]
    heads = []
    for h in range(GROUP):
        n = s * GROUP + h
        if h % 2 == 0:
            at = h // 2 * 128
            q = pq[:, at : at + 128].astype(BF16)
            kt = unit_keys[:, at : at + 128].T
            g0 = mm(q[:half], kt[:, :half])
            g1 = mm(q[half:], kt)
            qf = q.astype(F32)
        c, _, d00, d10, d11 = decays(n, cumul, cols)
        s00 = (d00 * g0).astype(BF16)
        s1 = jnp.concatenate(
            [(d10 * g1[:, :half]).astype(BF16), (d11 * g1[:, half:]).astype(BF16)], axis=1
        )
        heads.append((s00, s1, jnp.exp(c) * qf))
    for h, (s00, s1, eq) in enumerate(heads):
        solved = solved_ref[h]
        out0 = mm(s00, solved[:half])
        out1 = mm(s1, solved)
        at = h * 128
        rows_ref[0, :half, at : at + 128] = (eq[:half] - out0[:, 128:]).astype(BF16)
        rows_ref[0, half:, at : at + 128] = (eq[half:] - out1[:, 128:]).astype(BF16)
        rows_ref[1, :half, at : at + 128] = out0[:, :128].astype(BF16)
        rows_ref[1, half:, at : at + 128] = out1[:, :128].astype(BF16)


def local_rows(s, *args):
    tokens = args[0].shape[0]
    return small_call(
        functools.partial(rows_kernel, s), [(2, tokens, GROUP * 128)], args, "local_rows"
    )[0]


def small_call(kernel, outs, args, name, scratch=()):
    return pl.pallas_call(
        kernel,
        in_specs=[VMEM] * len(args),
        out_specs=[VMEM] * len(outs),
        out_shape=[jax.ShapeDtypeStruct(shape, BF16) for shape in outs],
        scratch_shapes=list(scratch),
        compiler_params=pltpu.CompilerParams(vmem_limit_bytes=16 * 1024 * 1024),
        name=name,
    )(*args)


def compose_kernel(keep, other, *outs):
    core, chip = place()
    first = core == 0
    for shift, out in enumerate(outs):
        for i in range(out.shape[0]):
            h = (chip + shift) % XS * out.shape[0] + i
            mine, theirs = keep[h], other[h]
            early = jnp.where(first, mine, theirs)
            late = jnp.where(first, theirs, mine)
            prod = mm(late[0], jnp.concatenate([early[0], early[1]], axis=1))
            out[i, 0] = prod[:, :128].astype(BF16)
            out[i, 1] = (prod[:, 128:] + late[1].astype(F32)).astype(BF16)


def advance(trans, state, extra):
    hi = state.astype(BF16)
    low = (state - hi.astype(F32)).astype(BF16)
    prod = mm(trans, jnp.concatenate([hi, low], axis=1))
    return prod[:, :128] + prod[:, 128:] + extra.astype(F32)


def total_kernel(*refs):
    parts, (ordered, total) = refs[:XS], refs[XS:]
    _, chip = place()
    for shift, part in enumerate(parts):
        ordered[(chip + XS - shift) % XS] = part[...]
    for i in range(total.shape[0]):
        state = ordered[0, i, 1].astype(F32)
        for j in range(1, XS):
            state = advance(ordered[j, i, 0], state, ordered[j, i, 1])
        total[i] = state.astype(BF16)


def starts_kernel(ordered, before, _, *refs):
    outs, scratch = refs[:XS], refs[XS]
    _, chip = place()
    for i in range(before.shape[0]):
        state = before[i].astype(F32)
        for j in range(XS):
            scratch[(j + XS - chip) % XS, i] = state.astype(BF16)
            if j + 1 < XS:
                state = advance(ordered[j, i, 0], state, ordered[j, i, 1])
    for shift, out in enumerate(outs):
        out[...] = scratch[shift]


def finish_head(rows_ref, rows_at, state, x_ref, x_at, gain):
    cols = pl.ds(pl.multiple_of(rows_at, 128), 128)
    mixed = mm(rows_ref[0, :, cols], state) + rows_ref[1, :, cols].astype(F32)
    scaled = mixed * lax.rsqrt(jnp.mean(mixed * mixed, axis=-1, keepdims=True) + EPS) * gain
    rows = x_ref[:, pl.ds(pl.multiple_of(x_at, 128), 128)].astype(F32)
    return (rows + scaled.astype(BF16).astype(F32)).astype(BF16)


def looked_after(parts, shifts, keep, other):
    core, chip = place()
    first = core == 0
    at = 0
    for shift, part in zip(shifts, parts):
        for i in range(part.shape[0]):
            h = (chip + XS - shift) % XS * part.shape[0] + i
            early = jnp.where(first, keep[h], other[h])
            start = part[i]
            after = (mm(early[0], start) + early[1].astype(F32)).astype(BF16)
            yield at, h, jnp.where(first, start, after), jnp.where(first, after, start)
            at += 128


def near_heads(parts, shifts, keep, other, near, x_ref, gain_ref, out_ref):
    core, _ = place()
    mid = x_ref.shape[1] // 2
    for at, h, mine, _ in looked_after(parts, shifts, keep, other):
        out_ref[:, at : at + 128] = finish_head(
            near, h * 128, mine, x_ref, core * mid + h * 128, gain_ref[...]
        )


def near_own_kernel(part, *refs):
    near_heads([part], [0], *refs)


def near_rest_kernel(*refs):
    near_heads(refs[: XS - 1], range(1, XS), *refs[XS - 1 :])


def theirs_kernel(*refs):
    parts, (keep, other, _, theirs) = refs[:XS], refs[XS:]
    for _, h, _, state in looked_after(parts, range(XS), keep, other):
        theirs[h] = state


def far_kernel(first, far, got, x_ref, gain_ref, _, out_ref):
    core, _ = place()
    mid = x_ref.shape[1] // 2
    for n in range(out_ref.shape[1] // 128):
        at = (first + n) * 128
        out_ref[:, n * 128 : n * 128 + 128] = finish_head(
            far, at, got[first + n], x_ref, (1 - core) * mid + at, gain_ref[...]
        )


def place_kernel(own, rest, far1, far2, out_hbm, sems):
    core, chip = place()
    mid = out_hbm.shape[1] // 2
    per = own.shape[1]

    def columns(at, size):
        return out_hbm.at[:, pl.ds(pl.multiple_of(at, 128), size)]

    there = (1 - core) * mid
    pairs = [(own, columns(core * mid + chip * per, per))]
    for shift in range(1, XS):
        part = rest.at[:, pl.ds((shift - 1) * per, per)]
        pairs.append((part, columns(core * mid + (chip + XS - shift) % XS * per, per)))
    pairs.append((far1, columns(there, far1.shape[1])))
    pairs.append((far2, columns(there + far1.shape[1], far2.shape[1])))
    for copy in fetch(pairs, sems):
        copy.wait()


def place_columns(width, *parts):
    return pl.pallas_call(
        place_kernel,
        in_specs=[VMEM] * len(parts),
        out_specs=pl.BlockSpec(memory_space=pltpu.HBM),
        out_shape=jax.ShapeDtypeStruct((parts[0].shape[0], width), BF16),
        scratch_shapes=[pltpu.SemaphoreType.DMA((XS + 2,))],
        compiler_params=pltpu.CompilerParams(vmem_limit_bytes=16 * 1024 * 1024),
        name="place_columns",
    )(*parts)


def swap_cores(array):
    return lax.ppermute(array, "ctx", [(i, i ^ 1) for i in range(lax.axis_size("ctx"))])


def along_x(array, shift):
    pairs = []
    for i in range(lax.axis_size("ctx")):
        row, chip, core = i // (2 * XS), i // 2 % XS, i % 2
        pairs.append((i, (row * XS + (chip + shift) % XS) * 2 + core))
    return lax.ppermute(array, "ctx", pairs)


def row_starts(keep, other, near):
    per = keep.shape[0] // XS
    parts = small_call(compose_kernel, [(per, 2, 128, 128)] * XS, (keep, other), "compose")
    parts = [parts[0]] + [along_x(parts[r], r) for r in range(1, XS)]
    ordered, total = small_call(
        total_kernel, [(XS, per, 2, 128, 128), (per, 128, 128)], parts, "row_total"
    )
    row = 2 * XS
    before = lax.ppermute(total, "ctx", [(i, i + row) for i in range(row)])
    starts = small_call(
        starts_kernel,
        [(per, 128, 128)] * XS,
        (ordered, before, near),
        "row_starts",
        [pltpu.VMEM((XS, per, 128, 128), BF16)],
    )
    return starts[0], [along_x(starts[r], r) for r in range(1, XS)]


def next_section(array):
    n = lax.axis_size("section")
    return lax.ppermute(array, "section", [(i, (i + 1) % n) for i in range(n)])


def on_device(layer_input, qk_weight, norm_gain, out_gain, log_decay, write_rate):
    send, far_keys, far_solved, x, normed, wk, wq, cumul, cols = first_pairs(
        layer_input[0], qk_weight[0], norm_gain, log_decay[0], write_rate[0]
    )
    other = swap_cores(send)
    keep, near_keys, near_solved = last_pairs(normed, wk, cumul, cols)
    near = local_rows(1, normed, wq, near_keys, near_solved, cumul, cols)
    far = local_rows(0, normed, wq, far_keys, far_solved, cumul, cols)
    own, rest = row_starts(keep, other, near)
    tokens, width = x.shape
    per = width // 2 // XS
    common = (keep, other, near, x, out_gain)
    done_own = small_call(near_own_kernel, [(tokens, per)], (own, *common), "finish_own")[0]
    done_own = next_section(done_own)
    done_rest = small_call(
        near_rest_kernel, [(tokens, (XS - 1) * per)], (*rest, *common), "finish_rest"
    )[0]
    done_rest = next_section(done_rest)
    theirs = small_call(
        theirs_kernel,
        [(keep.shape[0], 128, 128)],
        (own, *rest, keep, other, done_own),
        "other_core",
    )[0]
    got = swap_cores(theirs)

    def finish_far(first, after):
        done = small_call(
            functools.partial(far_kernel, first),
            [(tokens, width // 4)],
            (far, got, x, out_gain, after),
            "finish_far",
        )[0]
        return next_section(done)

    done_far1 = finish_far(0, done_own)
    done_far2 = finish_far(keep.shape[0] // 2, done_rest)
    return place_columns(width, done_own, done_rest, done_far1, done_far2)[None]


def solution(mesh):
    in_specs = (
        P("section", "ctx", None),
        P("section", None, None),
        P("section", None),
        P("section", None),
        P("section", None, "ctx"),
        P("section", None, "ctx"),
    )
    out_specs = P("section", "ctx", None)
    return jax.shard_map(
        on_device, mesh=mesh, in_specs=in_specs, out_specs=out_specs, check_vma=False
    )
```

profile of v0, /device:TPU:16, one launch (start us, length us, event | category | flops | bytes accessed | tf_op | source)
XLA Modules:
  0.0 66.0 jit_solution(17800587707436806820)
XLA Ops:
  0.0 5.4 %first_pairs.1 = (bf16[8,2,128,128]{3,2,1,0:T(8,128)(2,1)S(1)}, bf16[256,512]{1,0:T(8,128)(2,1)S(1)}, bf16[8,256,256]{2,1,0:T(8,128)(2,1)S(1)}, bf16[256,2048]{1...) custom-call(bf16[256,2048]{1,0:T(8,128)(2,1)} %bitcast.6, ...), custom_call_target="tpu_custom_call" | custom-call | flops 5000000000 | bytes 8000000 | tf_op jit(solution)/shard_map/first_pairs/pallas_call | solution.py:252
  5.4 0.1 collective-permute-start
  5.5 3.3 %last_pairs.1 = (bf16[8,2,128,128]{3,2,1,0:T(8,128)(2,1)S(1)}, bf16[256,512]{1,0:T(8,128)(2,1)S(1)}, bf16[8,256,256]{2,1,0:T(8,128)(2,1)S(1)}) custom-call(bf16[256,2048]{1,0:T(8,128)(2,1)S(1)} %get-tuple-element.27.normed, bf16[2,2048,512]{2,1,0:T(8,128)(2,1)S(1)} %get-tuple-element.28.wk, f32[16,256]{1,0:T(8,128)S(1)} %get-tuple-element.29.cumul_ref, ...), custom_call_target="tpu_custom_call" | custom-call | flops 5000000000 | bytes 8000000 | tf_op jit(solution)/shard_map/last_pairs/pallas_call | solution.py:252
  8.8 0.0 collective-permute-done.other.refs_1_.refs_4_.refs_5_
  8.9 0.3 compose.1
  9.2 1.6 %collective-permute-start.1 = (bf16[2,2,128,128]{3,2,1,0:T(8,128)(2,1)S(1)}, bf16[2,2,128,128]{3,2,1,0:T(8,128)(2,1)S(1)}, u32[]{:S(2)}, u32[]{:S(2)}) collective-permute-start(bf16[2,2,128,128]{3,2,1,0:T(8,128)(2,1)S(1)} %get-tuple-element.34), channel_id=1, source_target_pairs={{0,2},{1,3},{2,4},{3,5},{4,6},{5,7},{6,0},{7,1},{8,10},{9,11},{10,... | collective-permute-start | bytes 393224 | tf_op jit(solution)/shard_map/ppermute | solution.py:499
  10.8 2.7 %collective-permute-start.2 = (bf16[2,2,128,128]{3,2,1,0:T(8,128)(2,1)S(1)}, bf16[2,2,128,128]{3,2,1,0:T(8,128)(2,1)S(1)}, u32[]{:S(2)}, u32[]{:S(2)}) collective-permute-start(bf16[2,2,128,128]{3,2,1,0:T(8,128)(2,1)S(1)} %get-tuple-element.35), channel_id=1, source_target_pairs={{0,4},{1,5},{2,6},{3,7},{4,0},{5,1},{6,2},{7,3},{8,12},{9,13},{10,... | collective-permute-start | bytes 393224 | tf_op jit(solution)/shard_map/ppermute | solution.py:499
  13.5 1.4 %collective-permute-start.3 = (bf16[2,2,128,128]{3,2,1,0:T(8,128)(2,1)S(1)}, bf16[2,2,128,128]{3,2,1,0:T(8,128)(2,1)S(1)}, u32[]{:S(2)}, u32[]{:S(2)}) collective-permute-start(bf16[2,2,128,128]{3,2,1,0:T(8,128)(2,1)S(1)} %get-tuple-element.36), channel_id=1, source_target_pairs={{0,6},{1,7},{2,0},{3,1},{4,2},{5,3},{6,4},{7,5},{8,14},{9,15},{10,... | collective-permute-start | bytes 393224 | tf_op jit(solution)/shard_map/ppermute | solution.py:499
  14.9 1.5 %collective-permute-done.1.refs_1_ = bf16[2,2,128,128]{3,2,1,0:T(8,128)(2,1)S(1)} collective-permute-done((bf16[2,2,128,128]{3,2,1,0:T(8,128)(2,1)S(1)}, bf16[2,2,128,128]{3,2,1,0:T(8,128)(2,1)S(1)}, u32[]{:S(2)}, u32[]{:S(2)}) %collective-permute-start.1) | collective-permute-done | bytes 131104 | tf_op jit(solution)/shard_map/ppermute | solution.py:499
  16.4 3.8 %collective-permute-done.2.refs_2_ = bf16[2,2,128,128]{3,2,1,0:T(8,128)(2,1)S(1)} collective-permute-done((bf16[2,2,128,128]{3,2,1,0:T(8,128)(2,1)S(1)}, bf16[2,2,128,128]{3,2,1,0:T(8,128)(2,1)S(1)}, u32[]{:S(2)}, u32[]{:S(2)}) %collective-permute-start.2) | collective-permute-done | bytes 131104 | tf_op jit(solution)/shard_map/ppermute | solution.py:499
  20.2 0.0 collective-permute-done.3.refs_3_
  20.2 0.7 %row_total.1 = (bf16[4,2,2,128,128]{4,3,2,1,0:T(8,128)(2,1)S(1)}, bf16[2,128,128]{2,1,0:T(8,128)(2,1)S(1)}) custom-call(bf16[2,2,128,128]{3,2,1,0:T(8,128)(2,1)S(1)} %get-tuple-element.33.refs_0_, bf16[2,2,128,128]{3,2,1,0:T(8,128)(2,1)S(1)} %collective-permute-done.1.refs_1_, bf16[2,2,128,128]{3,2,1,0:T(8,128)(2,1)S(1)} %collective-permute-done.2.refs_2_, ...), custom_call_target="tpu_custom_call" | custom-call | tf_op jit(solution)/shard_map/row_total/pallas_call | solution.py:347
  20.9 1.3 %collective-permute-start.4 = (bf16[2,128,128]{2,1,0:T(8,128)(2,1)S(1)}, bf16[2,128,128]{2,1,0:T(8,128)(2,1)S(1)}, u32[]{:S(2)}, u32[]{:S(2)}) collective-permute-start(bf16[2,128,128]{2,1,0:T(8,128)(2,1)S(1)} %get-tuple-element.38), channel_id=1, source_target_pairs={{0,8},{1,9},{2,10},{3,11},{4,12},{5,13},{6,14},{7,15},{16,24},{17,... | collective-permute-start | bytes 196616 | tf_op jit(solution)/shard_map/ppermute | solution.py:510
  22.2 0.0 copy-start
  22.2 1.3 %local_rows.2._.refs_2_.refs_5_ = bf16[2,256,1024]{2,1,0:T(8,128)(2,1)S(1)} custom-call(bf16[256,2048]{1,0:T(8,128)(2,1)S(1)} %get-tuple-element.27.normed, bf16[2,2048,512]{2,1,0:T(8,128)(2,1)S(1)} %get-tuple-element.39.wq, bf16[256,512]{1,0:T(8,128)(2,1)S(1)} %get-tuple-element.40.unit_keys, bf16[8,256,256]{2,1,0:T(8,128)(2,1)S(1)} %get-tuple-element.41.solved_ref, ...), custom_call_target="tpu_custom_call" | custom-call | tf_op jit(solution)/shard_map/local_rows/pallas_call | solution.py:347
  23.5 5.0 %collective-permute-done.4.before = bf16[2,128,128]{2,1,0:T(8,128)(2,1)S(1)} collective-permute-done((bf16[2,128,128]{2,1,0:T(8,128)(2,1)S(1)}, bf16[2,128,128]{2,1,0:T(8,128)(2,1)S(1)}, u32[]{:S(2)}, u32[]{:S(2)}) %collective-permute-start.4) | collective-permute-done | bytes 65568 | tf_op jit(solution)/shard_map/ppermute | solution.py:510
  28.6 0.7 %row_starts.1 = (bf16[2,128,128]{2,1,0:T(8,128)(2,1)S(1)}, bf16[2,128,128]{2,1,0:T(8,128)(2,1)S(1)}, bf16[2,128,128]{2,1,0:T(8,128)(2,1)S(1)}, bf16[2,128,128]{2,1,0:T(8,128)(2,1)S(1)}) custom-call(bf16[4,2,2,128,128]{4,3,2,1,0:T(8,128)(2,1)S(1)} %get-tuple-element.37.ordered, bf16[2,128,128]{2,1,0:T(8,128)(2,1)S(1)} %collective-permute-done.4.before, ...), custom_call_target="tpu_custom_call" | custom-call | tf_op jit(solution)/shard_map/row_starts/pallas_call | solution.py:347
  29.3 1.6 %collective-permute-start.6 = (bf16[2,128,128]{2,1,0:T(8,128)(2,1)S(1)}, bf16[2,128,128]{2,1,0:T(8,128)(2,1)S(1)}, u32[]{:S(2)}, u32[]{:S(2)}) collective-permute-start(bf16[2,128,128]{2,1,0:T(8,128)(2,1)S(1)} %get-tuple-element.44), channel_id=1, source_target_pairs={{0,2},{1,3},{2,4},{3,5},{4,6},{5,7},{6,0},{7,1},{8,10},{9,11},{10,... | collective-permute-start | bytes 196616 | tf_op jit(solution)/shard_map/ppermute | solution.py:499
  30.8 2.4 %collective-permute-start.7 = (bf16[2,128,128]{2,1,0:T(8,128)(2,1)S(1)}, bf16[2,128,128]{2,1,0:T(8,128)(2,1)S(1)}, u32[]{:S(2)}, u32[]{:S(2)}) collective-permute-start(bf16[2,128,128]{2,1,0:T(8,128)(2,1)S(1)} %get-tuple-element.45), channel_id=1, source_target_pairs={{0,4},{1,5},{2,6},{3,7},{4,0},{5,1},{6,2},{7,3},{8,12},{9,13},{10,... | collective-permute-start | bytes 196616 | tf_op jit(solution)/shard_map/ppermute | solution.py:499
  33.2 1.6 %collective-permute-start.8 = (bf16[2,128,128]{2,1,0:T(8,128)(2,1)S(1)}, bf16[2,128,128]{2,1,0:T(8,128)(2,1)S(1)}, u32[]{:S(2)}, u32[]{:S(2)}) collective-permute-start(bf16[2,128,128]{2,1,0:T(8,128)(2,1)S(1)} %get-tuple-element.46), channel_id=1, source_target_pairs={{0,6},{1,7},{2,0},{3,1},{4,2},{5,3},{6,4},{7,5},{8,14},{9,15},{10,... | collective-permute-start | bytes 196616 | tf_op jit(solution)/shard_map/ppermute | solution.py:499
  34.8 0.0 copy-done
  34.8 0.5 finish_own.1
  35.3 2.0 %collective-permute-start.5 = (bf16[256,256]{1,0:T(8,128)(2,1)S(1)}, bf16[256,256]{1,0:T(8,128)(2,1)S(1)}, u32[]{:S(2)}, u32[]{:S(2)}) collective-permute-start(bf16[256,256]{1,0:T(8,128)(2,1)S(1)} %finish_own.1), channel_id=1, source_target_pairs={{0,16},{16,32},{32,48},{48,64},{64,80},{80,96},{96,112},{112,128},... | collective-permute-start | bytes 393224 | tf_op jit(solution)/shard_map/ppermute | solution.py:523
  37.3 0.0 collective-permute-done.6.refs_0_.refs_1_
  37.3 0.0 collective-permute-done.7.refs_1_.refs_2_
  37.3 0.2 collective-permute-done.8.refs_2_.refs_3_
  37.5 0.9 %finish_rest.1 = bf16[256,768]{1,0:T(8,128)(2,1)S(1)} custom-call(bf16[2,128,128]{2,1,0:T(8,128)(2,1)S(1)} %collective-permute-done.6.refs_0_.refs_1_, bf16[2,128,128]{2,1,0:T(8,128)(2,1)S(1)} %collective-permute-done.7.refs_1_.refs_2_, bf16[2,128,128]{2,1,0:T(8,128)(2,1)S(1)} %collective-permute-done.8.refs_2_.refs_3_, ...), custom_call_target="tpu_custom_call" | custom-call | tf_op jit(solution)/shard_map/finish_rest/pallas_call | solution.py:347
  38.4 2.0 %collective-permute-start.9 = (bf16[256,768]{1,0:T(8,128)(2,1)S(1)}, bf16[256,768]{1,0:T(8,128)(2,1)S(1)}, u32[]{:S(2)}, u32[]{:S(2)}) collective-permute-start(bf16[256,768]{1,0:T(8,128)(2,1)S(1)} %finish_rest.1), channel_id=1, source_target_pairs={{0,16},{16,32},{32,48},{48,64},{64,80},{80,96},{96,112},{112,128},... | collective-permute-start | bytes 1179656 | tf_op jit(solution)/shard_map/ppermute | solution.py:523
  40.4 5.8 %collective-permute-done.5.refs_6_._.own = bf16[256,256]{1,0:T(8,128)(2,1)S(1)} collective-permute-done((bf16[256,256]{1,0:T(8,128)(2,1)S(1)}, bf16[256,256]{1,0:T(8,128)(2,1)S(1)}, u32[]{:S(2)}, u32[]{:S(2)}) %collective-permute-start.5) | collective-permute-done | bytes 131104 | tf_op jit(solution)/shard_map/ppermute | solution.py:523
  46.2 0.2 other_core.1
  46.4 0.1 collective-permute-start.10
  46.5 1.3 %local_rows.3.far = bf16[2,256,1024]{2,1,0:T(8,128)(2,1)S(1)} custom-call(bf16[256,2048]{1,0:T(8,128)(2,1)S(1)} %get-tuple-element.27.normed, bf16[2,2048,512]{2,1,0:T(8,128)(2,1)S(1)} %get-tuple-element.39.wq, bf16[256,512]{1,0:T(8,128)(2,1)S(1)} %get-tuple-element.47.unit_keys, bf16[8,256,256]{2,1,0:T(8,128)(2,1)S(1)} %get-tuple-element.48.solved_ref, ...), custom_call_target="tpu_custom_call" | custom-call | tf_op jit(solution)/shard_map/local_rows/pallas_call | solution.py:347
  47.9 0.2 collective-permute-done.10.got
  48.0 0.4 finish_far.2
  48.5 0.1 collective-permute-start.11
  48.5 4.4 %collective-permute-done.9._.rest = bf16[256,768]{1,0:T(8,128)(2,1)S(1)} collective-permute-done((bf16[256,768]{1,0:T(8,128)(2,1)S(1)}, bf16[256,768]{1,0:T(8,128)(2,1)S(1)}, u32[]{:S(2)}, u32[]{:S(2)}) %collective-permute-start.9) | collective-permute-done | bytes 393248 | tf_op jit(solution)/shard_map/ppermute | solution.py:523
  52.9 0.4 finish_far.3
  53.3 0.1 collective-permute-start.12
  53.4 6.4 %collective-permute-done.11.far1 = bf16[256,512]{1,0:T(8,128)(2,1)S(1)} collective-permute-done((bf16[256,512]{1,0:T(8,128)(2,1)S(1)}, bf16[256,512]{1,0:T(8,128)(2,1)S(1)}, u32[]{:S(2)}, u32[]{:S(2)}) %collective-permute-start.11) | collective-permute-done | bytes 262176 | tf_op jit(solution)/shard_map/ppermute | solution.py:523
  59.8 5.0 %collective-permute-done.12.far2 = bf16[256,512]{1,0:T(8,128)(2,1)S(1)} collective-permute-done((bf16[256,512]{1,0:T(8,128)(2,1)S(1)}, bf16[256,512]{1,0:T(8,128)(2,1)S(1)}, u32[]{:S(2)}, u32[]{:S(2)}) %collective-permute-start.12) | collective-permute-done | bytes 262176 | tf_op jit(solution)/shard_map/ppermute | solution.py:523
  64.8 1.0 %place_columns.1 = bf16[256,2048]{1,0:T(8,128)(2,1)} custom-call(bf16[256,256]{1,0:T(8,128)(2,1)S(1)} %collective-permute-done.5.refs_6_._.own, bf16[256,768]{1,0:T(8,128)(2,1)S(1)} %collective-permute-done.9._.rest, bf16[256,512]{1,0:T(8,128)(2,1)S(1)} %collective-permute-done.11.far1, bf16[256,512]{1,0:T(8,128)(2,1)S(1)} %collective-permute-done.12.far2), custom_call_target="tpu_custom_call" | custom-call | tf_op jit(solution)/shard_map/place_columns/pallas_call | solution.py:479
Async XLA Ops:
  5.4 3.4 %collective-permute-start = (bf16[8,2,128,128]{3,2,1,0:T(8,128)(2,1)S(1)}, bf16[8,2,128,128]{3,2,1,0:T(8,128)(2,1)S(1)}, u32[]{:S(2)}, u32[]{:S(2)}) collective-permute-start(bf16[8,2,128,128]{3,2,1,0:T(8,128)(2,1)S(1)} %get-tuple-element.32), channel_id=1, source_target_pairs={{0,1},{1,0},{2,3},{3,2},{4,5},{5,4},{6,7},{7,6},{8,9},{9,8},{10,11... | collective-permute-start | bytes 1572872 | tf_op jit(solution)/shard_map/ppermute | solution.py:491
  9.2 7.2 %collective-permute-start.1 = (bf16[2,2,128,128]{3,2,1,0:T(8,128)(2,1)S(1)}, bf16[2,2,128,128]{3,2,1,0:T(8,128)(2,1)S(1)}, u32[]{:S(2)}, u32[]{:S(2)}) collective-permute-start(bf16[2,2,128,128]{3,2,1,0:T(8,128)(2,1)S(1)} %get-tuple-element.34), channel_id=1, source_target_pairs={{0,2},{1,3},{2,4},{3,5},{4,6},{5,7},{6,0},{7,1},{8,10},{9,11},{10,... | collective-permute-start | bytes 393224 | tf_op jit(solution)/shard_map/ppermute | solution.py:499
  10.8 9.4 %collective-permute-start.2 = (bf16[2,2,128,128]{3,2,1,0:T(8,128)(2,1)S(1)}, bf16[2,2,128,128]{3,2,1,0:T(8,128)(2,1)S(1)}, u32[]{:S(2)}, u32[]{:S(2)}) collective-permute-start(bf16[2,2,128,128]{3,2,1,0:T(8,128)(2,1)S(1)} %get-tuple-element.35), channel_id=1, source_target_pairs={{0,4},{1,5},{2,6},{3,7},{4,0},{5,1},{6,2},{7,3},{8,12},{9,13},{10,... | collective-permute-start | bytes 393224 | tf_op jit(solution)/shard_map/ppermute | solution.py:499
  13.5 6.7 %collective-permute-start.3 = (bf16[2,2,128,128]{3,2,1,0:T(8,128)(2,1)S(1)}, bf16[2,2,128,128]{3,2,1,0:T(8,128)(2,1)S(1)}, u32[]{:S(2)}, u32[]{:S(2)}) collective-permute-start(bf16[2,2,128,128]{3,2,1,0:T(8,128)(2,1)S(1)} %get-tuple-element.36), channel_id=1, source_target_pairs={{0,6},{1,7},{2,0},{3,1},{4,2},{5,3},{6,4},{7,5},{8,14},{9,15},{10,... | collective-permute-start | bytes 393224 | tf_op jit(solution)/shard_map/ppermute | solution.py:499
  20.9 7.7 %collective-permute-start.4 = (bf16[2,128,128]{2,1,0:T(8,128)(2,1)S(1)}, bf16[2,128,128]{2,1,0:T(8,128)(2,1)S(1)}, u32[]{:S(2)}, u32[]{:S(2)}) collective-permute-start(bf16[2,128,128]{2,1,0:T(8,128)(2,1)S(1)} %get-tuple-element.38), channel_id=1, source_target_pairs={{0,8},{1,9},{2,10},{3,11},{4,12},{5,13},{6,14},{7,15},{16,24},{17,... | collective-permute-start | bytes 196616 | tf_op jit(solution)/shard_map/ppermute | solution.py:510
  22.2 12.6 %copy-start = (f32[1,128]{1,0:T(1,128)S(1)}, f32[1,128]{1,0:T(1,128)}, u32[]{:S(2)}) copy-start(f32[1,128]{1,0:T(1,128)} %gain_ref.3) | copy-start | bytes 1540
  29.3 8.0 %collective-permute-start.6 = (bf16[2,128,128]{2,1,0:T(8,128)(2,1)S(1)}, bf16[2,128,128]{2,1,0:T(8,128)(2,1)S(1)}, u32[]{:S(2)}, u32[]{:S(2)}) collective-permute-start(bf16[2,128,128]{2,1,0:T(8,128)(2,1)S(1)} %get-tuple-element.44), channel_id=1, source_target_pairs={{0,2},{1,3},{2,4},{3,5},{4,6},{5,7},{6,0},{7,1},{8,10},{9,11},{10,... | collective-permute-start | bytes 196616 | tf_op jit(solution)/shard_map/ppermute | solution.py:499
  30.8 6.4 %collective-permute-start.7 = (bf16[2,128,128]{2,1,0:T(8,128)(2,1)S(1)}, bf16[2,128,128]{2,1,0:T(8,128)(2,1)S(1)}, u32[]{:S(2)}, u32[]{:S(2)}) collective-permute-start(bf16[2,128,128]{2,1,0:T(8,128)(2,1)S(1)} %get-tuple-element.45), channel_id=1, source_target_pairs={{0,4},{1,5},{2,6},{3,7},{4,0},{5,1},{6,2},{7,3},{8,12},{9,13},{10,... | collective-permute-start | bytes 196616 | tf_op jit(solution)/shard_map/ppermute | solution.py:499
  33.2 4.3 %collective-permute-start.8 = (bf16[2,128,128]{2,1,0:T(8,128)(2,1)S(1)}, bf16[2,128,128]{2,1,0:T(8,128)(2,1)S(1)}, u32[]{:S(2)}, u32[]{:S(2)}) collective-permute-start(bf16[2,128,128]{2,1,0:T(8,128)(2,1)S(1)} %get-tuple-element.46), channel_id=1, source_target_pairs={{0,6},{1,7},{2,0},{3,1},{4,2},{5,3},{6,4},{7,5},{8,14},{9,15},{10,... | collective-permute-start | bytes 196616 | tf_op jit(solution)/shard_map/ppermute | solution.py:499
  35.3 10.9 %collective-permute-start.5 = (bf16[256,256]{1,0:T(8,128)(2,1)S(1)}, bf16[256,256]{1,0:T(8,128)(2,1)S(1)}, u32[]{:S(2)}, u32[]{:S(2)}) collective-permute-start(bf16[256,256]{1,0:T(8,128)(2,1)S(1)} %finish_own.1), channel_id=1, source_target_pairs={{0,16},{16,32},{32,48},{48,64},{64,80},{80,96},{96,112},{112,128},... | collective-permute-start | bytes 393224 | tf_op jit(solution)/shard_map/ppermute | solution.py:523
  38.4 14.5 %collective-permute-start.9 = (bf16[256,768]{1,0:T(8,128)(2,1)S(1)}, bf16[256,768]{1,0:T(8,128)(2,1)S(1)}, u32[]{:S(2)}, u32[]{:S(2)}) collective-permute-start(bf16[256,768]{1,0:T(8,128)(2,1)S(1)} %finish_rest.1), channel_id=1, source_target_pairs={{0,16},{16,32},{32,48},{48,64},{64,80},{80,96},{96,112},{112,128},... | collective-permute-start | bytes 1179656 | tf_op jit(solution)/shard_map/ppermute | solution.py:523
  46.4 1.6 %collective-permute-start.10 = (bf16[8,128,128]{2,1,0:T(8,128)(2,1)S(1)}, bf16[8,128,128]{2,1,0:T(8,128)(2,1)S(1)}, u32[]{:S(2)}, u32[]{:S(2)}) collective-permute-start(bf16[8,128,128]{2,1,0:T(8,128)(2,1)S(1)} %other_core.1), channel_id=1, source_target_pairs={{0,1},{1,0},{2,3},{3,2},{4,5},{5,4},{6,7},{7,6},{8,9},{9,8},{10,11... | collective-permute-start | bytes 786440 | tf_op jit(solution)/shard_map/ppermute | solution.py:491
  48.5 11.3 %collective-permute-start.11 = (bf16[256,512]{1,0:T(8,128)(2,1)S(1)}, bf16[256,512]{1,0:T(8,128)(2,1)S(1)}, u32[]{:S(2)}, u32[]{:S(2)}) collective-permute-start(bf16[256,512]{1,0:T(8,128)(2,1)S(1)} %finish_far.2), channel_id=1, source_target_pairs={{0,16},{16,32},{32,48},{48,64},{64,80},{80,96},{96,112},{112,128},... | collective-permute-start | bytes 786440 | tf_op jit(solution)/shard_map/ppermute | solution.py:523
  53.3 11.5 %collective-permute-start.12 = (bf16[256,512]{1,0:T(8,128)(2,1)S(1)}, bf16[256,512]{1,0:T(8,128)(2,1)S(1)}, u32[]{:S(2)}, u32[]{:S(2)}) collective-permute-start(bf16[256,512]{1,0:T(8,128)(2,1)S(1)} %finish_far.3), channel_id=1, source_target_pairs={{0,16},{16,32},{32,48},{48,64},{64,80},{80,96},{96,112},{112,128},... | collective-permute-start | bytes 786440 | tf_op jit(solution)/shard_map/ppermute | solution.py:523
where the time goes:
time: 66.1 us; the launch traced here: 66 us
  waiting for transfers between devices  32.2 us (49%)
  starting transfers between devices  16.9 us (26%)
  Pallas kernels  16.5 us (25%)
    ppermute x4, waiting for transfers between devices, next_section(): return lax.ppermute(array, 'section', [(i, (i + 1) % n) for i in range(n)])  21.5 us
    ppermute x6, starting transfers between devices, along_x(): return lax.ppermute(array, 'ctx', pairs)  11.3 us
    pallas_call x2, Pallas kernels, pairs_call(): pl.pallas_call(kernel, in_specs=in_specs, out_specs=[VMEM] * len(outs), o...  8.73 us
    pallas_call x10, Pallas kernels, small_call(): pl.pallas_call(kernel, in_specs=[VMEM] * len(args), out_specs=[VMEM] * le...  6.81 us
    ppermute x6, waiting for transfers between devices, along_x(): return lax.ppermute(array, 'ctx', pairs)  5.48 us
    ppermute x1, waiting for transfers between devices, row_starts(): before = lax.ppermute(total, 'ctx', [(i, i + row) for i in range(row)])  5.03 us
    ppermute x4, starting transfers between devices, next_section(): return lax.ppermute(array, 'section', [(i, (i + 1) % n) for i in range(n)])  4.16 us
  transfers between devices with their start and end apart: 13, of which 9 were waited for; matrix products, arithmetic and copies ran while one was open for 0% of the time, Pallas kernels for 13%

commit v1 on v0

--- a/solution.py
+++ b/solution.py
@@ -14,6 +14,7 @@
 BASE = 8
 GROUP = 8
 XS = 4
+SPLIT = 4
 VMEM = pl.BlockSpec(memory_space=pltpu.VMEM)
 
 
@@ -198,19 +199,26 @@
     core, _ = place()
     here = pl.multiple_of(core * mid_head, mid_head)
     there = pl.multiple_of((1 - core) * mid_head, mid_head)
-    pairs = [(x_hbm, xbuf), (gain_hbm, gains)]
+    pairs = [(gain_hbm, gains)]
     for at, frm in ((0, there), (mid_head, here)):
         pairs.append((decay_hbm.at[pl.ds(frm, mid_head)], logs_buf.at[pl.ds(at, mid_head)]))
         pairs.append((rate_hbm.at[pl.ds(frm, mid_head)], rates_buf.at[pl.ds(at, mid_head)]))
+    x_at = len(pairs)
+    rows = tokens // SPLIT
+    for r in range(0, tokens, rows):
+        pairs.append((x_hbm.at[pl.ds(r, rows)], xbuf.at[pl.ds(r, rows)]))
     w_at = len(pairs)
+    rows = width // SPLIT
     for base, to in ((width // 2, wk), (0, wq)):
         for s in range(steps):
             frm = (s * wcols + (1 - core) * (width // 4)) % (width // 2)
             frm = pl.multiple_of(base + frm, 128)
-            pairs.append((w_hbm.at[:, pl.ds(frm, wcols)], to.at[s]))
+            for r in range(0, width, rows):
+                part = w_hbm.at[pl.ds(r, rows), pl.ds(frm, wcols)]
+                pairs.append((part, to.at[s, pl.ds(r, rows)]))
     copies = fetch(pairs, sems)
 
-    for copy in copies[2:w_at]:
+    for copy in copies[:x_at]:
         copy.wait()
     upto = (iota((tokens, tokens), 0) <= iota((tokens, tokens), 1)).astype(BF16)
     hi, mid, low = split3(logs_buf[...])
@@ -219,17 +227,18 @@
     cumul_ref[...] = cumul
     cols_ref[...] = cols
 
-    copies[0].wait()
-    copies[1].wait()
-    for r in range(0, tokens, 64):
-        xf = xbuf[r : r + 64, :].astype(F32)
-        normed[r : r + 64, :] = (
+    rows = tokens // SPLIT
+    for n, r in enumerate(range(0, tokens, rows)):
+        copies[x_at + n].wait()
+        xf = xbuf[r : r + rows, :].astype(F32)
+        normed[r : r + rows, :] = (
             xf * lax.rsqrt(jnp.mean(xf * xf, axis=-1, keepdims=True) + EPS) * gains[...]
         ).astype(BF16)
 
-    copies[w_at].wait()
+    for copy in copies[w_at : w_at + SPLIT]:
+        copy.wait()
     group_pairs(0, normed, wk[0], cumul, cols, pairs_ref, unit_keys, solved_ref)
-    for copy in copies[w_at + 1 :]:
+    for copy in copies[w_at + SPLIT :]:
         copy.wait()
 
 
@@ -285,7 +294,7 @@
             pltpu.VMEM((1, width), F32),
             pltpu.VMEM((heads, tokens), F32),
             pltpu.VMEM((heads, tokens), F32),
-            pltpu.SemaphoreType.DMA((6 + 2 * steps,)),
+            pltpu.SemaphoreType.DMA((5 + (1 + 2 * steps) * SPLIT,)),
         ],
         "first_pairs",
         [in_hbm(a) for a in (x, gain_in, log_decay, write_rate, weight)],
@@ -369,11 +378,16 @@
             out[i, 1] = (prod[:, 128:] + late[1].astype(F32)).astype(BF16)
 
 
-def advance(trans, state, extra):
-    hi = state.astype(BF16)
-    low = (state - hi.astype(F32)).astype(BF16)
-    prod = mm(trans, jnp.concatenate([hi, low], axis=1))
-    return prod[:, :128] + prod[:, 128:] + extra.astype(F32)
+def advance(pairs, states):
+    his = [state.astype(BF16) for state in states]
+    both = [
+        jnp.concatenate([hi, (state - hi.astype(F32)).astype(BF16)], axis=1)
+        for hi, state in zip(his, states)
+    ]
+    prods = [mm(pair[0], b) for pair, b in zip(pairs, both)]
+    return [
+        prod[:, :128] + prod[:, 128:] + pair[1].astype(F32) for pair, prod in zip(pairs, prods)
+    ]
 
 
 def total_kernel(*refs):
@@ -381,55 +395,62 @@
     _, chip = place()
     for shift, part in enumerate(parts):
         ordered[(chip + XS - shift) % XS] = part[...]
-    for i in range(total.shape[0]):
-        state = ordered[0, i, 1].astype(F32)
-        for j in range(1, XS):
-            state = advance(ordered[j, i, 0], state, ordered[j, i, 1])
-        total[i] = state.astype(BF16)
+    per = total.shape[0]
+    states = [ordered[0, i, 1].astype(F32) for i in range(per)]
+    for j in range(1, XS):
+        states = advance([ordered[j, i] for i in range(per)], states)
+    for i in range(per):
+        total[i] = states[i].astype(BF16)
 
 
 def starts_kernel(ordered, before, _, *refs):
     outs, scratch = refs[:XS], refs[XS]
     _, chip = place()
-    for i in range(before.shape[0]):
-        state = before[i].astype(F32)
-        for j in range(XS):
-            scratch[(j + XS - chip) % XS, i] = state.astype(BF16)
-            if j + 1 < XS:
-                state = advance(ordered[j, i, 0], state, ordered[j, i, 1])
+    per = before.shape[0]
+    states = [before[i].astype(F32) for i in range(per)]
+    for j in range(XS):
+        for i in range(per):
+            scratch[(j + XS - chip) % XS, i] = states[i].astype(BF16)
+        if j + 1 < XS:
+            states = advance([ordered[j, i] for i in range(per)], states)
     for shift, out in enumerate(outs):
         out[...] = scratch[shift]
 
 
-def finish_head(rows_ref, rows_at, state, x_ref, x_at, gain):
-    cols = pl.ds(pl.multiple_of(rows_at, 128), 128)
-    mixed = mm(rows_ref[0, :, cols], state) + rows_ref[1, :, cols].astype(F32)
-    scaled = mixed * lax.rsqrt(jnp.mean(mixed * mixed, axis=-1, keepdims=True) + EPS) * gain
-    rows = x_ref[:, pl.ds(pl.multiple_of(x_at, 128), 128)].astype(F32)
-    return (rows + scaled.astype(BF16).astype(F32)).astype(BF16)
+def finish_heads(rows_ref, rows_at, states, x_ref, x_at, gain, out_ref):
+    where = [pl.ds(pl.multiple_of(at, 128), 128) for at in rows_at]
+    mixed = [mm(rows_ref[0, :, w], state) for w, state in zip(where, states)]
+    mixed = [m + rows_ref[1, :, w].astype(F32) for m, w in zip(mixed, where)]
+    scales = [lax.rsqrt(jnp.mean(m * m, axis=-1, keepdims=True) + EPS) for m in mixed]
+    for n, (m, scale, at) in enumerate(zip(mixed, scales, x_at)):
+        rows = x_ref[:, pl.ds(pl.multiple_of(at, 128), 128)].astype(F32)
+        branch = (m * scale * gain).astype(BF16).astype(F32)
+        out_ref[:, n * 128 : n * 128 + 128] = (rows + branch).astype(BF16)
 
 
 def looked_after(parts, shifts, keep, other):
     core, chip = place()
     first = core == 0
-    at = 0
+    heads, starts = [], []
     for shift, part in zip(shifts, parts):
         for i in range(part.shape[0]):
-            h = (chip + XS - shift) % XS * part.shape[0] + i
-            early = jnp.where(first, keep[h], other[h])
-            start = part[i]
-            after = (mm(early[0], start) + early[1].astype(F32)).astype(BF16)
-            yield at, h, jnp.where(first, start, after), jnp.where(first, after, start)
-            at += 128
+            heads.append((chip + XS - shift) % XS * part.shape[0] + i)
+            starts.append(part[i])
+    early = [jnp.where(first, keep[h], other[h]) for h in heads]
+    after = [mm(e[0], start) for e, start in zip(early, starts)]
+    after = [(a + e[1].astype(F32)).astype(BF16) for a, e in zip(after, early)]
+    mine = [jnp.where(first, a, b) for a, b in zip(starts, after)]
+    theirs = [jnp.where(first, b, a) for a, b in zip(starts, after)]
+    return heads, mine, theirs
 
 
 def near_heads(parts, shifts, keep, other, near, x_ref, gain_ref, out_ref):
     core, _ = place()
     mid = x_ref.shape[1] // 2
-    for at, h, mine, _ in looked_after(parts, shifts, keep, other):
-        out_ref[:, at : at + 128] = finish_head(
-            near, h * 128, mine, x_ref, core * mid + h * 128, gain_ref[...]
-        )
+    heads, mine, _ = looked_after(parts, shifts, keep, other)
+    rows_at = [h * 128 for h in heads]
+    x_at = [core * mid + h * 128 for h in heads]
+    finish_heads(near, rows_at, mine, x_ref, x_at, gain_ref[...], out_ref)
 
 
 def near_own_kernel(part, *refs):
@@ -442,21 +463,21 @@
 
 def theirs_kernel(*refs):
     parts, (keep, other, _, theirs) = refs[:XS], refs[XS:]
-    for _, h, _, state in looked_after(parts, range(XS), keep, other):
+    heads, _, states = looked_after(parts, range(XS), keep, other)
+    for h, state in zip(heads, states):
         theirs[h] = state
 
 
 def far_kernel(first, far, got, x_ref, gain_ref, _, out_ref):
     core, _ = place()
     mid = x_ref.shape[1] // 2
-    for n in range(out_ref.shape[1] // 128):
-        at = (first + n) * 128
-        out_ref[:, n * 128 : n * 128 + 128] = finish_head(
-            far, at, got[first + n], x_ref, (1 - core) * mid + at, gain_ref[...]
-        )
-
-
-def place_kernel(own, rest, far1, far2, out_hbm, sems):
+    heads = range(first, first + out_ref.shape[1] // 128)
+    rows_at = [h * 128 for h in heads]
+    x_at = [(1 - core) * mid + at for at in rows_at]
+    finish_heads(far, rows_at, [got[h] for h in heads], x_ref, x_at, gain_ref[...], out_ref)
+
+
+def place_kernel(own, rest, far1, out_hbm, sems):
     core, chip = place()
     mid = out_hbm.shape[1] // 2
     per = own.shape[1]
@@ -464,27 +485,36 @@
     def columns(at, size):
         return out_hbm.at[:, pl.ds(pl.multiple_of(at, 128), size)]
 
-    there = (1 - core) * mid
     pairs = [(own, columns(core * mid + chip * per, per))]
     for shift in range(1, XS):
         part = rest.at[:, pl.ds((shift - 1) * per, per)]
         pairs.append((part, columns(core * mid + (chip + XS - shift) % XS * per, per)))
-    pairs.append((far1, columns(there, far1.shape[1])))
-    pairs.append((far2, columns(there + far1.shape[1], far2.shape[1])))
+    pairs.append((far1, columns((1 - core) * mid, far1.shape[1])))
     for copy in fetch(pairs, sems):
         copy.wait()
 
 
-def place_columns(width, *parts):
+def place_last_kernel(far2, _, out_hbm, sems):
+    core, _ = place()
+    cols = far2.shape[1]
+    at = pl.multiple_of((1 - core) * 2 * cols + cols, 128)
+    for copy in fetch([(far2, out_hbm.at[:, pl.ds(at, cols)])], sems):
+        copy.wait()
+
+
+def place_columns(width, kernel, parts, name, out=None):
+    hbm = pl.BlockSpec(memory_space=pltpu.HBM)
+    last = () if out is None else (out,)
     return pl.pallas_call(
-        place_kernel,
-        in_specs=[VMEM] * len(parts),
-        out_specs=pl.BlockSpec(memory_space=pltpu.HBM),
+        kernel,
+        in_specs=[VMEM] * len(parts) + [hbm] * len(last),
+        out_specs=hbm,
         out_shape=jax.ShapeDtypeStruct((parts[0].shape[0], width), BF16),
-        scratch_shapes=[pltpu.SemaphoreType.DMA((XS + 2,))],
+        scratch_shapes=[pltpu.SemaphoreType.DMA((XS + 1,))],
+        input_output_aliases={len(parts): 0} if last else {},
         compiler_params=pltpu.CompilerParams(vmem_limit_bytes=16 * 1024 * 1024),
-        name="place_columns",
-    )(*parts)
+        name=name,
+    )(*parts, *last)
 
 
 def swap_cores(array):
@@ -560,7 +590,8 @@
 
     done_far1 = finish_far(0, done_own)
     done_far2 = finish_far(keep.shape[0] // 2, done_rest)
-    return place_columns(width, done_own, done_rest, done_far1, done_far2)[None]
+    most = place_columns(width, place_kernel, (done_own, done_rest, done_far1), "place_most")
+    return place_columns(width, place_last_kernel, (done_far2,), "place_last", most)[None]
 
 
 def solution(mesh):

time: 66.1 us -> 65.6 us (level)
  waiting for transfers between devices: 32.2 us -> 31.5 us
    ppermute x4, waiting for transfers between devices: 21.5 us -> 20.8 us  [next_section(): return lax.ppermute(array, 'section', [(i, (i + 1) % n) for i in range(n)])]
    pallas_call x1 -> x2, Pallas kernels: 1.01 us -> 1.66 us  [place_columns(): pl.pallas_call(kernel, in_specs=[VMEM] * len(parts) + [hbm] * len(last),...]
  transfers between devices with their start and end apart: 13 -> 13, of which waited for: 9 -> 9; matrix products, arithmetic and copies ran while one was open for 0% -> 0% of each run, Pallas kernels for 13% -> 14%
where the time goes in v1:
time: 65.6 us; the launch traced here: 65.5 us
  waiting for transfers between devices  31.5 us (48%)
  starting transfers between devices  16.9 us (26%)
  Pallas kernels  16.8 us (26%)
    ppermute x4, waiting for transfers between devices, next_section(): return lax.ppermute(array, 'section', [(i, (i + 1) % n) for i in range(n)])  20.8 us
    ppermute x6, starting transfers between devices, along_x(): return lax.ppermute(array, 'ctx', pairs)  11.3 us
    pallas_call x2, Pallas kernels, pairs_call(): pl.pallas_call(kernel, in_specs=in_specs, out_specs=[VMEM] * len(outs), o...  8.81 us
    pallas_call x10, Pallas kernels, small_call(): pl.pallas_call(kernel, in_specs=[VMEM] * len(args), out_specs=[VMEM] * le...  6.29 us
    ppermute x6, waiting for transfers between devices, along_x(): return lax.ppermute(array, 'ctx', pairs)  5.49 us
    ppermute x1, waiting for transfers between devices, row_starts(): before = lax.ppermute(total, 'ctx', [(i, i + row) for i in range(row)])  5.03 us
    ppermute x4, starting transfers between devices, next_section(): return lax.ppermute(array, 'section', [(i, (i + 1) % n) for i in range(n)])  4.14 us
    pallas_call x2, Pallas kernels, place_columns(): pl.pallas_call(kernel, in_specs=[VMEM] * len(parts) + [hbm] * len(last),...  1.66 us
  transfers between devices with their start and end apart: 13, of which 9 were waited for; matrix products, arithmetic and copies ran while one was open for 0% of the time, Pallas kernels for 14%

profile of v1, /device:TPU:16, one launch (start us, length us, event | category | flops | bytes accessed | tf_op | source)
XLA Modules:
  0.0 65.5 jit_solution(9009825899018729243)
XLA Ops:
  0.0 5.5 %first_pairs.1 = (bf16[8,2,128,128]{3,2,1,0:T(8,128)(2,1)S(1)}, bf16[256,512]{1,0:T(8,128)(2,1)S(1)}, bf16[8,256,256]{2,1,0:T(8,128)(2,1)S(1)}, bf16[256,2048]{1...) custom-call(bf16[256,2048]{1,0:T(8,128)(2,1)} %bitcast.6, ...), custom_call_target="tpu_custom_call" | custom-call | flops 5000000000 | bytes 8000000 | tf_op jit(solution)/shard_map/first_pairs/pallas_call | solution.py:261
  5.5 0.1 collective-permute-start
  5.6 3.3 %last_pairs.1 = (bf16[8,2,128,128]{3,2,1,0:T(8,128)(2,1)S(1)}, bf16[256,512]{1,0:T(8,128)(2,1)S(1)}, bf16[8,256,256]{2,1,0:T(8,128)(2,1)S(1)}) custom-call(bf16[256,2048]{1,0:T(8,128)(2,1)S(1)} %get-tuple-element.27.normed, bf16[2,2048,512]{2,1,0:T(8,128)(2,1)S(1)} %get-tuple-element.33.wk, f32[16,256]{1,0:T(8,128)S(1)} %get-tuple-element.31.cumul_ref, ...), custom_call_target="tpu_custom_call" | custom-call | flops 5000000000 | bytes 8000000 | tf_op jit(solution)/shard_map/last_pairs/pallas_call | solution.py:261
  8.9 0.0 collective-permute-done.other.refs_1_.refs_5_.refs_4_
  8.9 0.3 compose.1
  9.3 1.6 %collective-permute-start.1 = (bf16[2,2,128,128]{3,2,1,0:T(8,128)(2,1)S(1)}, bf16[2,2,128,128]{3,2,1,0:T(8,128)(2,1)S(1)}, u32[]{:S(2)}, u32[]{:S(2)}) collective-permute-start(bf16[2,2,128,128]{3,2,1,0:T(8,128)(2,1)S(1)} %get-tuple-element.37), channel_id=1, source_target_pairs={{0,2},{1,3},{2,4},{3,5},{4,6},{5,7},{6,0},{7,1},{8,10},{9,11},{10,... | collective-permute-start | bytes 393224 | tf_op jit(solution)/shard_map/ppermute | solution.py:529
  10.8 2.7 %collective-permute-start.2 = (bf16[2,2,128,128]{3,2,1,0:T(8,128)(2,1)S(1)}, bf16[2,2,128,128]{3,2,1,0:T(8,128)(2,1)S(1)}, u32[]{:S(2)}, u32[]{:S(2)}) collective-permute-start(bf16[2,2,128,128]{3,2,1,0:T(8,128)(2,1)S(1)} %get-tuple-element.38), channel_id=1, source_target_pairs={{0,4},{1,5},{2,6},{3,7},{4,0},{5,1},{6,2},{7,3},{8,12},{9,13},{10,... | collective-permute-start | bytes 393224 | tf_op jit(solution)/shard_map/ppermute | solution.py:529
  13.6 1.4 %collective-permute-start.3 = (bf16[2,2,128,128]{3,2,1,0:T(8,128)(2,1)S(1)}, bf16[2,2,128,128]{3,2,1,0:T(8,128)(2,1)S(1)}, u32[]{:S(2)}, u32[]{:S(2)}) collective-permute-start(bf16[2,2,128,128]{3,2,1,0:T(8,128)(2,1)S(1)} %get-tuple-element.39), channel_id=1, source_target_pairs={{0,6},{1,7},{2,0},{3,1},{4,2},{5,3},{6,4},{7,5},{8,14},{9,15},{10,... | collective-permute-start | bytes 393224 | tf_op jit(solution)/shard_map/ppermute | solution.py:529
  15.0 1.5 %collective-permute-done.1.refs_1_ = bf16[2,2,128,128]{3,2,1,0:T(8,128)(2,1)S(1)} collective-permute-done((bf16[2,2,128,128]{3,2,1,0:T(8,128)(2,1)S(1)}, bf16[2,2,128,128]{3,2,1,0:T(8,128)(2,1)S(1)}, u32[]{:S(2)}, u32[]{:S(2)}) %collective-permute-start.1) | collective-permute-done | bytes 131104 | tf_op jit(solution)/shard_map/ppermute | solution.py:529
  16.5 3.8 %collective-permute-done.2.refs_2_ = bf16[2,2,128,128]{3,2,1,0:T(8,128)(2,1)S(1)} collective-permute-done((bf16[2,2,128,128]{3,2,1,0:T(8,128)(2,1)S(1)}, bf16[2,2,128,128]{3,2,1,0:T(8,128)(2,1)S(1)}, u32[]{:S(2)}, u32[]{:S(2)}) %collective-permute-start.2) | collective-permute-done | bytes 131104 | tf_op jit(solution)/shard_map/ppermute | solution.py:529
  20.2 0.0 collective-permute-done.3.refs_3_
  20.2 0.6 row_total.1
  20.8 1.3 %collective-permute-start.4 = (bf16[2,128,128]{2,1,0:T(8,128)(2,1)S(1)}, bf16[2,128,128]{2,1,0:T(8,128)(2,1)S(1)}, u32[]{:S(2)}, u32[]{:S(2)}) collective-permute-start(bf16[2,128,128]{2,1,0:T(8,128)(2,1)S(1)} %get-tuple-element.41), channel_id=1, source_target_pairs={{0,8},{1,9},{2,10},{3,11},{4,12},{5,13},{6,14},{7,15},{16,24},{17,... | collective-permute-start | bytes 196616 | tf_op jit(solution)/shard_map/ppermute | solution.py:540
  22.1 0.0 copy-start
  22.1 1.3 %local_rows.3._.refs_2_.refs_5_ = bf16[2,256,1024]{2,1,0:T(8,128)(2,1)S(1)} custom-call(bf16[256,2048]{1,0:T(8,128)(2,1)S(1)} %get-tuple-element.27.normed, bf16[2,2048,512]{2,1,0:T(8,128)(2,1)S(1)} %get-tuple-element.28.wq, bf16[256,512]{1,0:T(8,128)(2,1)S(1)} %get-tuple-element.42.unit_keys, bf16[8,256,256]{2,1,0:T(8,128)(2,1)S(1)} %get-tuple-element.43.solved_ref, ...), custom_call_target="tpu_custom_call" | custom-call | tf_op jit(solution)/shard_map/local_rows/pallas_call | solution.py:356
  23.4 5.0 %collective-permute-done.4.before = bf16[2,128,128]{2,1,0:T(8,128)(2,1)S(1)} collective-permute-done((bf16[2,128,128]{2,1,0:T(8,128)(2,1)S(1)}, bf16[2,128,128]{2,1,0:T(8,128)(2,1)S(1)}, u32[]{:S(2)}, u32[]{:S(2)}) %collective-permute-start.4) | collective-permute-done | bytes 65568 | tf_op jit(solution)/shard_map/ppermute | solution.py:540
  28.5 0.5 row_starts.1
  29.0 1.6 %collective-permute-start.5 = (bf16[2,128,128]{2,1,0:T(8,128)(2,1)S(1)}, bf16[2,128,128]{2,1,0:T(8,128)(2,1)S(1)}, u32[]{:S(2)}, u32[]{:S(2)}) collective-permute-start(bf16[2,128,128]{2,1,0:T(8,128)(2,1)S(1)} %get-tuple-element.45), channel_id=1, source_target_pairs={{0,2},{1,3},{2,4},{3,5},{4,6},{5,7},{6,0},{7,1},{8,10},{9,11},{10,... | collective-permute-start | bytes 196616 | tf_op jit(solution)/shard_map/ppermute | solution.py:529
  30.6 2.4 %collective-permute-start.6 = (bf16[2,128,128]{2,1,0:T(8,128)(2,1)S(1)}, bf16[2,128,128]{2,1,0:T(8,128)(2,1)S(1)}, u32[]{:S(2)}, u32[]{:S(2)}) collective-permute-start(bf16[2,128,128]{2,1,0:T(8,128)(2,1)S(1)} %get-tuple-element.46), channel_id=1, source_target_pairs={{0,4},{1,5},{2,6},{3,7},{4,0},{5,1},{6,2},{7,3},{8,12},{9,13},{10,... | collective-permute-start | bytes 196616 | tf_op jit(solution)/shard_map/ppermute | solution.py:529
  33.0 1.6 %collective-permute-start.7 = (bf16[2,128,128]{2,1,0:T(8,128)(2,1)S(1)}, bf16[2,128,128]{2,1,0:T(8,128)(2,1)S(1)}, u32[]{:S(2)}, u32[]{:S(2)}) collective-permute-start(bf16[2,128,128]{2,1,0:T(8,128)(2,1)S(1)} %get-tuple-element.47), channel_id=1, source_target_pairs={{0,6},{1,7},{2,0},{3,1},{4,2},{5,3},{6,4},{7,5},{8,14},{9,15},{10,... | collective-permute-start | bytes 196616 | tf_op jit(solution)/shard_map/ppermute | solution.py:529
  34.6 0.0 copy-done
  34.6 0.5 finish_own.1
  35.0 2.0 %collective-permute-start.8 = (bf16[256,256]{1,0:T(8,128)(2,1)S(1)}, bf16[256,256]{1,0:T(8,128)(2,1)S(1)}, u32[]{:S(2)}, u32[]{:S(2)}) collective-permute-start(bf16[256,256]{1,0:T(8,128)(2,1)S(1)} %finish_own.1), channel_id=1, source_target_pairs={{0,16},{16,32},{32,48},{48,64},{64,80},{80,96},{96,112},{112,128},... | collective-permute-start | bytes 393224 | tf_op jit(solution)/shard_map/ppermute | solution.py:553
  37.0 0.0 collective-permute-done.5.refs_1_.refs_0_
  37.0 0.0 collective-permute-done.6.refs_2_.refs_1_
  37.0 0.2 collective-permute-done.7.refs_3_.refs_2_
  37.3 0.7 %finish_rest.1 = bf16[256,768]{1,0:T(8,128)(2,1)S(1)} custom-call(bf16[2,128,128]{2,1,0:T(8,128)(2,1)S(1)} %collective-permute-done.5.refs_1_.refs_0_, bf16[2,128,128]{2,1,0:T(8,128)(2,1)S(1)} %collective-permute-done.6.refs_2_.refs_1_, bf16[2,128,128]{2,1,0:T(8,128)(2,1)S(1)} %collective-permute-done.7.refs_3_.refs_2_, ...), custom_call_target="tpu_custom_call" | custom-call | tf_op jit(solution)/shard_map/finish_rest/pallas_call | solution.py:356
  38.0 2.0 %collective-permute-start.10 = (bf16[256,768]{1,0:T(8,128)(2,1)S(1)}, bf16[256,768]{1,0:T(8,128)(2,1)S(1)}, u32[]{:S(2)}, u32[]{:S(2)}) collective-permute-start(bf16[256,768]{1,0:T(8,128)(2,1)S(1)} %finish_rest.1), channel_id=1, source_target_pairs={{0,16},{16,32},{32,48},{48,64},{64,80},{80,96},{96,112},{112,128},... | collective-permute-start | bytes 1179656 | tf_op jit(solution)/shard_map/ppermute | solution.py:553
  40.0 6.0 %collective-permute-done.8.refs_6_._.own = bf16[256,256]{1,0:T(8,128)(2,1)S(1)} collective-permute-done((bf16[256,256]{1,0:T(8,128)(2,1)S(1)}, bf16[256,256]{1,0:T(8,128)(2,1)S(1)}, u32[]{:S(2)}, u32[]{:S(2)}) %collective-permute-start.8) | collective-permute-done | bytes 131104 | tf_op jit(solution)/shard_map/ppermute | solution.py:553
  46.0 0.2 other_core.1
  46.2 0.1 collective-permute-start.9
  46.3 1.3 %local_rows.2.far = bf16[2,256,1024]{2,1,0:T(8,128)(2,1)S(1)} custom-call(bf16[256,2048]{1,0:T(8,128)(2,1)S(1)} %get-tuple-element.27.normed, bf16[2,2048,512]{2,1,0:T(8,128)(2,1)S(1)} %get-tuple-element.28.wq, bf16[256,512]{1,0:T(8,128)(2,1)S(1)} %get-tuple-element.29.unit_keys, bf16[8,256,256]{2,1,0:T(8,128)(2,1)S(1)} %get-tuple-element.30.solved_ref, ...), custom_call_target="tpu_custom_call" | custom-call | tf_op jit(solution)/shard_map/local_rows/pallas_call | solution.py:356
  47.6 0.2 collective-permute-done.9.got
  47.8 0.4 finish_far.3
  48.3 0.1 collective-permute-start.12
  48.3 4.1 %collective-permute-done.10._.rest = bf16[256,768]{1,0:T(8,128)(2,1)S(1)} collective-permute-done((bf16[256,768]{1,0:T(8,128)(2,1)S(1)}, bf16[256,768]{1,0:T(8,128)(2,1)S(1)}, u32[]{:S(2)}, u32[]{:S(2)}) %collective-permute-start.10) | collective-permute-done | bytes 393248 | tf_op jit(solution)/shard_map/ppermute | solution.py:553
  52.5 0.4 finish_far.2
  52.9 0.1 collective-permute-start.11
  53.0 6.6 %collective-permute-done.12.far1 = bf16[256,512]{1,0:T(8,128)(2,1)S(1)} collective-permute-done((bf16[256,512]{1,0:T(8,128)(2,1)S(1)}, bf16[256,512]{1,0:T(8,128)(2,1)S(1)}, u32[]{:S(2)}, u32[]{:S(2)}) %collective-permute-start.12) | collective-permute-done | bytes 262176 | tf_op jit(solution)/shard_map/ppermute | solution.py:553
  59.6 0.9 %place_most.1._ = bf16[256,2048]{1,0:T(8,128)(2,1)} custom-call(bf16[256,256]{1,0:T(8,128)(2,1)S(1)} %collective-permute-done.8.refs_6_._.own, bf16[256,768]{1,0:T(8,128)(2,1)S(1)} %collective-permute-done.10._.rest, bf16[256,512]{1,0:T(8,128)(2,1)S(1)} %collective-permute-done.12.far1), custom_call_target="tpu_custom_call" | custom-call | tf_op jit(solution)/shard_map/place_most/pallas_call | solution.py:508
  60.5 4.1 %collective-permute-done.11.far2 = bf16[256,512]{1,0:T(8,128)(2,1)S(1)} collective-permute-done((bf16[256,512]{1,0:T(8,128)(2,1)S(1)}, bf16[256,512]{1,0:T(8,128)(2,1)S(1)}, u32[]{:S(2)}, u32[]{:S(2)}) %collective-permute-start.11) | collective-permute-done | bytes 262176 | tf_op jit(solution)/shard_map/ppermute | solution.py:553
  64.6 0.7 %place_last.1 = bf16[256,2048]{1,0:T(8,128)(2,1)} custom-call(bf16[256,512]{1,0:T(8,128)(2,1)S(1)} %collective-permute-done.11.far2, bf16[256,2048]{1,0:T(8,128)(2,1)} %place_most.1._), custom_call_target="tpu_custom_call", output_to_operand_aliasing={{}: (1, {})} | custom-call | tf_op jit(solution)/shard_map/place_last/pallas_call | solution.py:508
Async XLA Ops:
  5.5 3.4 %collective-permute-start = (bf16[8,2,128,128]{3,2,1,0:T(8,128)(2,1)S(1)}, bf16[8,2,128,128]{3,2,1,0:T(8,128)(2,1)S(1)}, u32[]{:S(2)}, u32[]{:S(2)}) collective-permute-start(bf16[8,2,128,128]{3,2,1,0:T(8,128)(2,1)S(1)} %get-tuple-element.35), channel_id=1, source_target_pairs={{0,1},{1,0},{2,3},{3,2},{4,5},{5,4},{6,7},{7,6},{8,9},{9,8},{10,11... | collective-permute-start | bytes 1572872 | tf_op jit(solution)/shard_map/ppermute | solution.py:521
  9.3 7.2 %collective-permute-start.1 = (bf16[2,2,128,128]{3,2,1,0:T(8,128)(2,1)S(1)}, bf16[2,2,128,128]{3,2,1,0:T(8,128)(2,1)S(1)}, u32[]{:S(2)}, u32[]{:S(2)}) collective-permute-start(bf16[2,2,128,128]{3,2,1,0:T(8,128)(2,1)S(1)} %get-tuple-element.37), channel_id=1, source_target_pairs={{0,2},{1,3},{2,4},{3,5},{4,6},{5,7},{6,0},{7,1},{8,10},{9,11},{10,... | collective-permute-start | bytes 393224 | tf_op jit(solution)/shard_map/ppermute | solution.py:529
  10.8 9.4 %collective-permute-start.2 = (bf16[2,2,128,128]{3,2,1,0:T(8,128)(2,1)S(1)}, bf16[2,2,128,128]{3,2,1,0:T(8,128)(2,1)S(1)}, u32[]{:S(2)}, u32[]{:S(2)}) collective-permute-start(bf16[2,2,128,128]{3,2,1,0:T(8,128)(2,1)S(1)} %get-tuple-element.38), channel_id=1, source_target_pairs={{0,4},{1,5},{2,6},{3,7},{4,0},{5,1},{6,2},{7,3},{8,12},{9,13},{10,... | collective-permute-start | bytes 393224 | tf_op jit(solution)/shard_map/ppermute | solution.py:529
  13.6 6.7 %collective-permute-start.3 = (bf16[2,2,128,128]{3,2,1,0:T(8,128)(2,1)S(1)}, bf16[2,2,128,128]{3,2,1,0:T(8,128)(2,1)S(1)}, u32[]{:S(2)}, u32[]{:S(2)}) collective-permute-start(bf16[2,2,128,128]{3,2,1,0:T(8,128)(2,1)S(1)} %get-tuple-element.39), channel_id=1, source_target_pairs={{0,6},{1,7},{2,0},{3,1},{4,2},{5,3},{6,4},{7,5},{8,14},{9,15},{10,... | collective-permute-start | bytes 393224 | tf_op jit(solution)/shard_map/ppermute | solution.py:529
  20.8 7.7 %collective-permute-start.4 = (bf16[2,128,128]{2,1,0:T(8,128)(2,1)S(1)}, bf16[2,128,128]{2,1,0:T(8,128)(2,1)S(1)}, u32[]{:S(2)}, u32[]{:S(2)}) collective-permute-start(bf16[2,128,128]{2,1,0:T(8,128)(2,1)S(1)} %get-tuple-element.41), channel_id=1, source_target_pairs={{0,8},{1,9},{2,10},{3,11},{4,12},{5,13},{6,14},{7,15},{16,24},{17,... | collective-permute-start | bytes 196616 | tf_op jit(solution)/shard_map/ppermute | solution.py:540
  22.1 12.5 %copy-start = (f32[1,128]{1,0:T(1,128)S(1)}, f32[1,128]{1,0:T(1,128)}, u32[]{:S(2)}) copy-start(f32[1,128]{1,0:T(1,128)} %gain_ref.3) | copy-start | bytes 1540
  29.0 8.0 %collective-permute-start.5 = (bf16[2,128,128]{2,1,0:T(8,128)(2,1)S(1)}, bf16[2,128,128]{2,1,0:T(8,128)(2,1)S(1)}, u32[]{:S(2)}, u32[]{:S(2)}) collective-permute-start(bf16[2,128,128]{2,1,0:T(8,128)(2,1)S(1)} %get-tuple-element.45), channel_id=1, source_target_pairs={{0,2},{1,3},{2,4},{3,5},{4,6},{5,7},{6,0},{7,1},{8,10},{9,11},{10,... | collective-permute-start | bytes 196616 | tf_op jit(solution)/shard_map/ppermute | solution.py:529
  30.6 6.4 %collective-permute-start.6 = (bf16[2,128,128]{2,1,0:T(8,128)(2,1)S(1)}, bf16[2,128,128]{2,1,0:T(8,128)(2,1)S(1)}, u32[]{:S(2)}, u32[]{:S(2)}) collective-permute-start(bf16[2,128,128]{2,1,0:T(8,128)(2,1)S(1)} %get-tuple-element.46), channel_id=1, source_target_pairs={{0,4},{1,5},{2,6},{3,7},{4,0},{5,1},{6,2},{7,3},{8,12},{9,13},{10,... | collective-permute-start | bytes 196616 | tf_op jit(solution)/shard_map/ppermute | solution.py:529
  33.0 4.3 %collective-permute-start.7 = (bf16[2,128,128]{2,1,0:T(8,128)(2,1)S(1)}, bf16[2,128,128]{2,1,0:T(8,128)(2,1)S(1)}, u32[]{:S(2)}, u32[]{:S(2)}) collective-permute-start(bf16[2,128,128]{2,1,0:T(8,128)(2,1)S(1)} %get-tuple-element.47), channel_id=1, source_target_pairs={{0,6},{1,7},{2,0},{3,1},{4,2},{5,3},{6,4},{7,5},{8,14},{9,15},{10,... | collective-permute-start | bytes 196616 | tf_op jit(solution)/shard_map/ppermute | solution.py:529
  35.0 10.9 %collective-permute-start.8 = (bf16[256,256]{1,0:T(8,128)(2,1)S(1)}, bf16[256,256]{1,0:T(8,128)(2,1)S(1)}, u32[]{:S(2)}, u32[]{:S(2)}) collective-permute-start(bf16[256,256]{1,0:T(8,128)(2,1)S(1)} %finish_own.1), channel_id=1, source_target_pairs={{0,16},{16,32},{32,48},{48,64},{64,80},{80,96},{96,112},{112,128},... | collective-permute-start | bytes 393224 | tf_op jit(solution)/shard_map/ppermute | solution.py:553
  38.0 14.5 %collective-permute-start.10 = (bf16[256,768]{1,0:T(8,128)(2,1)S(1)}, bf16[256,768]{1,0:T(8,128)(2,1)S(1)}, u32[]{:S(2)}, u32[]{:S(2)}) collective-permute-start(bf16[256,768]{1,0:T(8,128)(2,1)S(1)} %finish_rest.1), channel_id=1, source_target_pairs={{0,16},{16,32},{32,48},{48,64},{64,80},{80,96},{96,112},{112,128},... | collective-permute-start | bytes 1179656 | tf_op jit(solution)/shard_map/ppermute | solution.py:553
  46.2 1.6 %collective-permute-start.9 = (bf16[8,128,128]{2,1,0:T(8,128)(2,1)S(1)}, bf16[8,128,128]{2,1,0:T(8,128)(2,1)S(1)}, u32[]{:S(2)}, u32[]{:S(2)}) collective-permute-start(bf16[8,128,128]{2,1,0:T(8,128)(2,1)S(1)} %other_core.1), channel_id=1, source_target_pairs={{0,1},{1,0},{2,3},{3,2},{4,5},{5,4},{6,7},{7,6},{8,9},{9,8},{10,11... | collective-permute-start | bytes 786440 | tf_op jit(solution)/shard_map/ppermute | solution.py:521
  48.3 11.3 %collective-permute-start.12 = (bf16[256,512]{1,0:T(8,128)(2,1)S(1)}, bf16[256,512]{1,0:T(8,128)(2,1)S(1)}, u32[]{:S(2)}, u32[]{:S(2)}) collective-permute-start(bf16[256,512]{1,0:T(8,128)(2,1)S(1)} %finish_far.3), channel_id=1, source_target_pairs={{0,16},{16,32},{32,48},{48,64},{64,80},{80,96},{96,112},{112,128},... | collective-permute-start | bytes 786440 | tf_op jit(solution)/shard_map/ppermute | solution.py:553
  52.9 11.7 %collective-permute-start.11 = (bf16[256,512]{1,0:T(8,128)(2,1)S(1)}, bf16[256,512]{1,0:T(8,128)(2,1)S(1)}, u32[]{:S(2)}, u32[]{:S(2)}) collective-permute-start(bf16[256,512]{1,0:T(8,128)(2,1)S(1)} %finish_far.2), channel_id=1, source_target_pairs={{0,16},{16,32},{32,48},{48,64},{64,80},{80,96},{96,112},{112,128},... | collective-permute-start | bytes 786440 | tf_op jit(solution)/shard_map/ppermute | solution.py:553

commit v2 on v1

--- a/solution.py
+++ b/solution.py
@@ -367,15 +367,18 @@
 def compose_kernel(keep, other, *outs):
     core, chip = place()
     first = core == 0
+    slots, early, late = [], [], []
     for shift, out in enumerate(outs):
         for i in range(out.shape[0]):
             h = (chip + shift) % XS * out.shape[0] + i
             mine, theirs = keep[h], other[h]
-            early = jnp.where(first, mine, theirs)
-            late = jnp.where(first, theirs, mine)
-            prod = mm(late[0], jnp.concatenate([early[0], early[1]], axis=1))
-            out[i, 0] = prod[:, :128].astype(BF16)
-            out[i, 1] = (prod[:, 128:] + late[1].astype(F32)).astype(BF16)
+            slots.append((out, i))
+            early.append(jnp.where(first, mine, theirs))
+            late.append(jnp.where(first, theirs, mine))
+    prods = [mm(b[0], jnp.concatenate([a[0], a[1]], axis=1)) for a, b in zip(early, late)]
+    for (out, i), b, prod in zip(slots, late, prods):
+        out[i, 0] = prod[:, :128].astype(BF16)
+        out[i, 1] = (prod[:, 128:] + b[1].astype(F32)).astype(BF16)
 
 
 def advance(pairs, states):
@@ -391,7 +394,7 @@
 
 
 def total_kernel(*refs):
-    parts, (ordered, total) = refs[:XS], refs[XS:]
+    parts, (ordered, total) = refs[:XS], refs[XS + 1 :]
     _, chip = place()
     for shift, part in enumerate(parts):
         ordered[(chip + XS - shift) % XS] = part[...]
@@ -403,16 +406,45 @@
         total[i] = states[i].astype(BF16)
 
 
-def starts_kernel(ordered, before, _, *refs):
+def split2(value):
+    hi = value.astype(BF16)
+    return hi, (value - hi.astype(F32)).astype(BF16)
+
+
+def row_kernel(ordered, trans, state):
+    shape = trans.shape
+    per = shape[1]
+    pairs = [
+        jnp.concatenate([ordered[0, i, 0], ordered[0, i, 1]], axis=1).astype(F32)
+        for i in range(per)
+    ]
+    for j in range(shape[0]):
+        if j:
+            both = [jnp.concatenate(split2(p), axis=1) for p in pairs]
+            prods = [mm(ordered[j, i, 0], b) for i, b in enumerate(both)]
+            sums = [p[:, :256] + p[:, 256:] for p in prods]
+            pairs = [
+                jnp.concatenate([p[:, :128], p[:, 128:] + ordered[j, i, 1].astype(F32)], axis=1)
+                for i, p in enumerate(sums)
+            ]
+        for i, p in enumerate(pairs):
+            hi, low = split2(p)
+            trans[j, i, :128], trans[j, i, 128:] = hi[:, :128], low[:, :128]
+            state[j, i, :128], state[j, i, 128:] = hi[:, 128:], low[:, 128:]
+
+
+def starts_kernel(trans, state, before, _, *refs):
     outs, scratch = refs[:XS], refs[XS]
     _, chip = place()
     per = before.shape[0]
-    states = [before[i].astype(F32) for i in range(per)]
-    for j in range(XS):
-        for i in range(per):
-            scratch[(j + XS - chip) % XS, i] = states[i].astype(BF16)
-        if j + 1 < XS:
-            states = advance([ordered[j, i] for i in range(per)], states)
+    places = [(j, i) for j in range(XS - 1) for i in range(per)]
+    prods = [mm(trans[j, i], before[i]) for j, i in places]
+    for i in range(per):
+        scratch[(XS - chip) % XS, i] = before[i]
+    for (j, i), prod in zip(places, prods):
+        extra = state[j, i, :128].astype(F32) + state[j, i, 128:].astype(F32)
+        value = prod[:128] + prod[128:] + extra
+        scratch[(j + 1 + XS - chip) % XS, i] = value.astype(BF16)
     for shift, out in enumerate(outs):
         out[...] = scratch[shift]
 
@@ -529,19 +561,20 @@
     return lax.ppermute(array, "ctx", pairs)
 
 
-def row_starts(keep, other, near):
+def row_starts(keep, other, near, far):
     per = keep.shape[0] // XS
     parts = small_call(compose_kernel, [(per, 2, 128, 128)] * XS, (keep, other), "compose")
     parts = [parts[0]] + [along_x(parts[r], r) for r in range(1, XS)]
     ordered, total = small_call(
-        total_kernel, [(XS, per, 2, 128, 128), (per, 128, 128)], parts, "row_total"
+        total_kernel, [(XS, per, 2, 128, 128), (per, 128, 128)], (*parts, near), "row_total"
     )
     row = 2 * XS
     before = lax.ppermute(total, "ctx", [(i, i + row) for i in range(row)])
+    row_pairs = small_call(row_kernel, [(XS - 1, per, 256, 128)] * 2, (ordered,), "row_pairs")
     starts = small_call(
         starts_kernel,
         [(per, 128, 128)] * XS,
-        (ordered, before, near),
+        (*row_pairs, before, far),
         "row_starts",
         [pltpu.VMEM((XS, per, 128, 128), BF16)],
     )
@@ -561,7 +594,7 @@
     keep, near_keys, near_solved = last_pairs(normed, wk, cumul, cols)
     near = local_rows(1, normed, wq, near_keys, near_solved, cumul, cols)
     far = local_rows(0, normed, wq, far_keys, far_solved, cumul, cols)
-    own, rest = row_starts(keep, other, near)
+    own, rest = row_starts(keep, other, near, far)
     tokens, width = x.shape
     per = width // 2 // XS
     common = (keep, other, near, x, out_gain)

time: 65.6 us -> 65 us (level)
  waiting for transfers between devices: 31.5 us -> 30.7 us
    ppermute x2, waiting for transfers between devices: 0.19 us -> 1.52 us  [swap_cores(): lax.ppermute(array, 'ctx', [(i, i ^ 1) for i in range(lax.axis_size('ctx'...]
    ppermute x6, waiting for transfers between devices: 5.49 us -> 4.17 us  [along_x(): return lax.ppermute(array, 'ctx', pairs)]
    pallas_call x10 -> x11, Pallas kernels: 6.29 us -> 6.46 us  [small_call(): pl.pallas_call(kernel, in_specs=[VMEM] * len(args), out_specs=[VMEM] * le...]
  transfers between devices with their start and end apart: 13 -> 13, of which waited for: 9 -> 9; matrix products, arithmetic and copies ran while one was open for 0% -> 0% of each run, Pallas kernels for 14% -> 15%
where the time goes in v2:
time: 65 us; the launch traced here: 64.9 us
  waiting for transfers between devices  30.7 us (47%)
  Pallas kernels  16.9 us (26%)
  starting transfers between devices  16.9 us (26%)
    ppermute x4, waiting for transfers between devices, next_section(): return lax.ppermute(array, 'section', [(i, (i + 1) % n) for i in range(n)])  20.6 us
    ppermute x6, starting transfers between devices, along_x(): return lax.ppermute(array, 'ctx', pairs)  11.1 us
    pallas_call x2, Pallas kernels, pairs_call(): pl.pallas_call(kernel, in_specs=in_specs, out_specs=[VMEM] * len(outs), o...  8.81 us
    pallas_call x11, Pallas kernels, small_call(): pl.pallas_call(kernel, in_specs=[VMEM] * len(args), out_specs=[VMEM] * le...  6.46 us
    ppermute x1, waiting for transfers between devices, row_starts(): before = lax.ppermute(total, 'ctx', [(i, i + row) for i in range(row)])  4.39 us
    ppermute x6, waiting for transfers between devices, along_x(): return lax.ppermute(array, 'ctx', pairs)  4.17 us
    ppermute x4, starting transfers between devices, next_section(): return lax.ppermute(array, 'section', [(i, (i + 1) % n) for i in range(n)])  4.14 us
    pallas_call x2, Pallas kernels, place_columns(): pl.pallas_call(kernel, in_specs=[VMEM] * len(parts) + [hbm] * len(last),...  1.66 us
  transfers between devices with their start and end apart: 13, of which 9 were waited for; matrix products, arithmetic and copies ran while one was open for 0% of the time, Pallas kernels for 15%

profile of v2, /device:TPU:16, one launch (start us, length us, event | category | flops | bytes accessed | tf_op | source)
XLA Modules:
  0.0 64.9 jit_solution(5819466996808777149)
XLA Ops:
  0.0 5.5 %first_pairs.1 = (bf16[8,2,128,128]{3,2,1,0:T(8,128)(2,1)S(1)}, bf16[256,512]{1,0:T(8,128)(2,1)S(1)}, bf16[8,256,256]{2,1,0:T(8,128)(2,1)S(1)}, bf16[256,2048]{1...) custom-call(bf16[256,2048]{1,0:T(8,128)(2,1)} %bitcast.6, ...), custom_call_target="tpu_custom_call" | custom-call | flops 5000000000 | bytes 8000000 | tf_op jit(solution)/shard_map/first_pairs/pallas_call | solution.py:261
  5.5 0.1 collective-permute-start
  5.6 3.3 %last_pairs.1 = (bf16[8,2,128,128]{3,2,1,0:T(8,128)(2,1)S(1)}, bf16[256,512]{1,0:T(8,128)(2,1)S(1)}, bf16[8,256,256]{2,1,0:T(8,128)(2,1)S(1)}) custom-call(bf16[256,2048]{1,0:T(8,128)(2,1)S(1)} %get-tuple-element.29.normed, bf16[2,2048,512]{2,1,0:T(8,128)(2,1)S(1)} %get-tuple-element.35.wk, f32[16,256]{1,0:T(8,128)S(1)} %get-tuple-element.33.cumul_ref, ...), custom_call_target="tpu_custom_call" | custom-call | flops 5000000000 | bytes 8000000 | tf_op jit(solution)/shard_map/last_pairs/pallas_call | solution.py:261
  8.9 0.0 collective-permute-done.other.refs_1_.refs_5_.refs_4_
  8.9 0.3 compose.1
  9.3 1.6 %collective-permute-start.1 = (bf16[2,2,128,128]{3,2,1,0:T(8,128)(2,1)S(1)}, bf16[2,2,128,128]{3,2,1,0:T(8,128)(2,1)S(1)}, u32[]{:S(2)}, u32[]{:S(2)}) collective-permute-start(bf16[2,2,128,128]{3,2,1,0:T(8,128)(2,1)S(1)} %get-tuple-element.39), channel_id=1, source_target_pairs={{0,2},{1,3},{2,4},{3,5},{4,6},{5,7},{6,0},{7,1},{8,10},{9,11},{10,... | collective-permute-start | bytes 393224 | tf_op jit(solution)/shard_map/ppermute | solution.py:561
  10.8 2.7 %collective-permute-start.2 = (bf16[2,2,128,128]{3,2,1,0:T(8,128)(2,1)S(1)}, bf16[2,2,128,128]{3,2,1,0:T(8,128)(2,1)S(1)}, u32[]{:S(2)}, u32[]{:S(2)}) collective-permute-start(bf16[2,2,128,128]{3,2,1,0:T(8,128)(2,1)S(1)} %get-tuple-element.40), channel_id=1, source_target_pairs={{0,4},{1,5},{2,6},{3,7},{4,0},{5,1},{6,2},{7,3},{8,12},{9,13},{10,... | collective-permute-start | bytes 393224 | tf_op jit(solution)/shard_map/ppermute | solution.py:561
  13.6 1.4 %collective-permute-start.3 = (bf16[2,2,128,128]{3,2,1,0:T(8,128)(2,1)S(1)}, bf16[2,2,128,128]{3,2,1,0:T(8,128)(2,1)S(1)}, u32[]{:S(2)}, u32[]{:S(2)}) collective-permute-start(bf16[2,2,128,128]{3,2,1,0:T(8,128)(2,1)S(1)} %get-tuple-element.41), channel_id=1, source_target_pairs={{0,6},{1,7},{2,0},{3,1},{4,2},{5,3},{6,4},{7,5},{8,14},{9,15},{10,... | collective-permute-start | bytes 393224 | tf_op jit(solution)/shard_map/ppermute | solution.py:561
  15.0 1.3 %local_rows.3.refs_4_.refs_2_.refs_5_ = bf16[2,256,1024]{2,1,0:T(8,128)(2,1)S(1)} custom-call(bf16[256,2048]{1,0:T(8,128)(2,1)S(1)} %get-tuple-element.29.normed, bf16[2,2048,512]{2,1,0:T(8,128)(2,1)S(1)} %get-tuple-element.30.wq, bf16[256,512]{1,0:T(8,128)(2,1)S(1)} %get-tuple-element.42.unit_keys, bf16[8,256,256]{2,1,0:T(8,128)(2,1)S(1)} %get-tuple-element.43.solved_ref, ...), custom_call_target="tpu_custom_call" | custom-call | tf_op jit(solution)/shard_map/local_rows/pallas_call | solution.py:356
  16.3 0.1 collective-permute-done.1.refs_1_
  16.5 3.8 %collective-permute-done.2.refs_2_ = bf16[2,2,128,128]{3,2,1,0:T(8,128)(2,1)S(1)} collective-permute-done((bf16[2,2,128,128]{3,2,1,0:T(8,128)(2,1)S(1)}, bf16[2,2,128,128]{3,2,1,0:T(8,128)(2,1)S(1)}, u32[]{:S(2)}, u32[]{:S(2)}) %collective-permute-start.2) | collective-permute-done | bytes 131104 | tf_op jit(solution)/shard_map/ppermute | solution.py:561
  20.2 0.0 collective-permute-done.3.refs_3_
  20.2 0.6 row_total.1
  20.8 1.5 %collective-permute-start.4 = (bf16[2,128,128]{2,1,0:T(8,128)(2,1)S(1)}, bf16[2,128,128]{2,1,0:T(8,128)(2,1)S(1)}, u32[]{:S(2)}, u32[]{:S(2)}) collective-permute-start(bf16[2,128,128]{2,1,0:T(8,128)(2,1)S(1)} %get-tuple-element.47), channel_id=1, source_target_pairs={{0,8},{1,9},{2,10},{3,11},{4,12},{5,13},{6,14},{7,15},{16,24},{17,... | collective-permute-start | bytes 196616 | tf_op jit(solution)/shard_map/ppermute | solution.py:572
  22.3 0.0 copy-start
  22.3 1.3 %local_rows.2._.far = bf16[2,256,1024]{2,1,0:T(8,128)(2,1)S(1)} custom-call(bf16[256,2048]{1,0:T(8,128)(2,1)S(1)} %get-tuple-element.29.normed, bf16[2,2048,512]{2,1,0:T(8,128)(2,1)S(1)} %get-tuple-element.30.wq, bf16[256,512]{1,0:T(8,128)(2,1)S(1)} %get-tuple-element.31.unit_keys, bf16[8,256,256]{2,1,0:T(8,128)(2,1)S(1)} %get-tuple-element.32.solved_ref, ...), custom_call_target="tpu_custom_call" | custom-call | tf_op jit(solution)/shard_map/local_rows/pallas_call | solution.py:356
  23.6 0.4 row_pairs.1
  24.1 4.4 %collective-permute-done.4.before = bf16[2,128,128]{2,1,0:T(8,128)(2,1)S(1)} collective-permute-done((bf16[2,128,128]{2,1,0:T(8,128)(2,1)S(1)}, bf16[2,128,128]{2,1,0:T(8,128)(2,1)S(1)}, u32[]{:S(2)}, u32[]{:S(2)}) %collective-permute-start.4) | collective-permute-done | bytes 65568 | tf_op jit(solution)/shard_map/ppermute | solution.py:572
  28.5 0.3 row_starts.1
  28.8 1.4 %collective-permute-start.5 = (bf16[2,128,128]{2,1,0:T(8,128)(2,1)S(1)}, bf16[2,128,128]{2,1,0:T(8,128)(2,1)S(1)}, u32[]{:S(2)}, u32[]{:S(2)}) collective-permute-start(bf16[2,128,128]{2,1,0:T(8,128)(2,1)S(1)} %get-tuple-element.49), channel_id=1, source_target_pairs={{0,2},{1,3},{2,4},{3,5},{4,6},{5,7},{6,0},{7,1},{8,10},{9,11},{10,... | collective-permute-start | bytes 196616 | tf_op jit(solution)/shard_map/ppermute | solution.py:561
  30.2 2.4 %collective-permute-start.6 = (bf16[2,128,128]{2,1,0:T(8,128)(2,1)S(1)}, bf16[2,128,128]{2,1,0:T(8,128)(2,1)S(1)}, u32[]{:S(2)}, u32[]{:S(2)}) collective-permute-start(bf16[2,128,128]{2,1,0:T(8,128)(2,1)S(1)} %get-tuple-element.50), channel_id=1, source_target_pairs={{0,4},{1,5},{2,6},{3,7},{4,0},{5,1},{6,2},{7,3},{8,12},{9,13},{10,... | collective-permute-start | bytes 196616 | tf_op jit(solution)/shard_map/ppermute | solution.py:561
  32.6 1.6 %collective-permute-start.7 = (bf16[2,128,128]{2,1,0:T(8,128)(2,1)S(1)}, bf16[2,128,128]{2,1,0:T(8,128)(2,1)S(1)}, u32[]{:S(2)}, u32[]{:S(2)}) collective-permute-start(bf16[2,128,128]{2,1,0:T(8,128)(2,1)S(1)} %get-tuple-element.51), channel_id=1, source_target_pairs={{0,6},{1,7},{2,0},{3,1},{4,2},{5,3},{6,4},{7,5},{8,14},{9,15},{10,... | collective-permute-start | bytes 196616 | tf_op jit(solution)/shard_map/ppermute | solution.py:561
  34.1 0.0 copy-done
  34.1 0.5 finish_own.1
  34.6 2.0 %collective-permute-start.8 = (bf16[256,256]{1,0:T(8,128)(2,1)S(1)}, bf16[256,256]{1,0:T(8,128)(2,1)S(1)}, u32[]{:S(2)}, u32[]{:S(2)}) collective-permute-start(bf16[256,256]{1,0:T(8,128)(2,1)S(1)} %finish_own.1), channel_id=1, source_target_pairs={{0,16},{16,32},{32,48},{48,64},{64,80},{80,96},{96,112},{112,128},... | collective-permute-start | bytes 393224 | tf_op jit(solution)/shard_map/ppermute | solution.py:586
  36.6 0.0 collective-permute-done.5.refs_1_.refs_0_
  36.6 0.0 collective-permute-done.6.refs_2_.refs_1_
  36.6 0.2 collective-permute-done.7.refs_3_.refs_2_
  36.8 0.7 %finish_rest.1 = bf16[256,768]{1,0:T(8,128)(2,1)S(1)} custom-call(bf16[2,128,128]{2,1,0:T(8,128)(2,1)S(1)} %collective-permute-done.5.refs_1_.refs_0_, bf16[2,128,128]{2,1,0:T(8,128)(2,1)S(1)} %collective-permute-done.6.refs_2_.refs_1_, bf16[2,128,128]{2,1,0:T(8,128)(2,1)S(1)} %collective-permute-done.7.refs_3_.refs_2_, ...), custom_call_target="tpu_custom_call" | custom-call | tf_op jit(solution)/shard_map/finish_rest/pallas_call | solution.py:356
  37.6 2.0 %collective-permute-start.10 = (bf16[256,768]{1,0:T(8,128)(2,1)S(1)}, bf16[256,768]{1,0:T(8,128)(2,1)S(1)}, u32[]{:S(2)}, u32[]{:S(2)}) collective-permute-start(bf16[256,768]{1,0:T(8,128)(2,1)S(1)} %finish_rest.1), channel_id=1, source_target_pairs={{0,16},{16,32},{32,48},{48,64},{64,80},{80,96},{96,112},{112,128},... | collective-permute-start | bytes 1179656 | tf_op jit(solution)/shard_map/ppermute | solution.py:586
  39.6 6.0 %collective-permute-done.8.refs_6_._.own = bf16[256,256]{1,0:T(8,128)(2,1)S(1)} collective-permute-done((bf16[256,256]{1,0:T(8,128)(2,1)S(1)}, bf16[256,256]{1,0:T(8,128)(2,1)S(1)}, u32[]{:S(2)}, u32[]{:S(2)}) %collective-permute-start.8) | collective-permute-done | bytes 131104 | tf_op jit(solution)/shard_map/ppermute | solution.py:586
  45.5 0.2 other_core.1
  45.8 0.1 collective-permute-start.9
  45.9 1.5 %collective-permute-done.9.got = bf16[8,128,128]{2,1,0:T(8,128)(2,1)S(1)} collective-permute-done((bf16[8,128,128]{2,1,0:T(8,128)(2,1)S(1)}, bf16[8,128,128]{2,1,0:T(8,128)(2,1)S(1)}, u32[]{:S(2)}, u32[]{:S(2)}) %collective-permute-start.9) | collective-permute-done | bytes 262176 | tf_op jit(solution)/shard_map/ppermute | solution.py:553
  47.4 0.4 finish_far.3
  47.8 0.1 collective-permute-start.12
  47.9 4.1 %collective-permute-done.10._.rest = bf16[256,768]{1,0:T(8,128)(2,1)S(1)} collective-permute-done((bf16[256,768]{1,0:T(8,128)(2,1)S(1)}, bf16[256,768]{1,0:T(8,128)(2,1)S(1)}, u32[]{:S(2)}, u32[]{:S(2)}) %collective-permute-start.10) | collective-permute-done | bytes 393248 | tf_op jit(solution)/shard_map/ppermute | solution.py:586
  52.0 0.4 finish_far.2
  52.5 0.1 collective-permute-start.11
  52.5 6.6 %collective-permute-done.12.far1 = bf16[256,512]{1,0:T(8,128)(2,1)S(1)} collective-permute-done((bf16[256,512]{1,0:T(8,128)(2,1)S(1)}, bf16[256,512]{1,0:T(8,128)(2,1)S(1)}, u32[]{:S(2)}, u32[]{:S(2)}) %collective-permute-start.12) | collective-permute-done | bytes 262176 | tf_op jit(solution)/shard_map/ppermute | solution.py:586
  59.1 0.9 %place_most.1._ = bf16[256,2048]{1,0:T(8,128)(2,1)} custom-call(bf16[256,256]{1,0:T(8,128)(2,1)S(1)} %collective-permute-done.8.refs_6_._.own, bf16[256,768]{1,0:T(8,128)(2,1)S(1)} %collective-permute-done.10._.rest, bf16[256,512]{1,0:T(8,128)(2,1)S(1)} %collective-permute-done.12.far1), custom_call_target="tpu_custom_call" | custom-call | tf_op jit(solution)/shard_map/place_most/pallas_call | solution.py:540
  60.1 3.9 %collective-permute-done.11.far2 = bf16[256,512]{1,0:T(8,128)(2,1)S(1)} collective-permute-done((bf16[256,512]{1,0:T(8,128)(2,1)S(1)}, bf16[256,512]{1,0:T(8,128)(2,1)S(1)}, u32[]{:S(2)}, u32[]{:S(2)}) %collective-permute-start.11) | collective-permute-done | bytes 262176 | tf_op jit(solution)/shard_map/ppermute | solution.py:586
  64.0 0.7 %place_last.1 = bf16[256,2048]{1,0:T(8,128)(2,1)} custom-call(bf16[256,512]{1,0:T(8,128)(2,1)S(1)} %collective-permute-done.11.far2, bf16[256,2048]{1,0:T(8,128)(2,1)} %place_most.1._), custom_call_target="tpu_custom_call", output_to_operand_aliasing={{}: (1, {})} | custom-call | tf_op jit(solution)/shard_map/place_last/pallas_call | solution.py:540
Async XLA Ops:
  5.5 3.4 %collective-permute-start = (bf16[8,2,128,128]{3,2,1,0:T(8,128)(2,1)S(1)}, bf16[8,2,128,128]{3,2,1,0:T(8,128)(2,1)S(1)}, u32[]{:S(2)}, u32[]{:S(2)}) collective-permute-start(bf16[8,2,128,128]{3,2,1,0:T(8,128)(2,1)S(1)} %get-tuple-element.37), channel_id=1, source_target_pairs={{0,1},{1,0},{2,3},{3,2},{4,5},{5,4},{6,7},{7,6},{8,9},{9,8},{10,11... | collective-permute-start | bytes 1572872 | tf_op jit(solution)/shard_map/ppermute | solution.py:553
  9.3 7.2 %collective-permute-start.1 = (bf16[2,2,128,128]{3,2,1,0:T(8,128)(2,1)S(1)}, bf16[2,2,128,128]{3,2,1,0:T(8,128)(2,1)S(1)}, u32[]{:S(2)}, u32[]{:S(2)}) collective-permute-start(bf16[2,2,128,128]{3,2,1,0:T(8,128)(2,1)S(1)} %get-tuple-element.39), channel_id=1, source_target_pairs={{0,2},{1,3},{2,4},{3,5},{4,6},{5,7},{6,0},{7,1},{8,10},{9,11},{10,... | collective-permute-start | bytes 393224 | tf_op jit(solution)/shard_map/ppermute | solution.py:561
  10.8 9.4 %collective-permute-start.2 = (bf16[2,2,128,128]{3,2,1,0:T(8,128)(2,1)S(1)}, bf16[2,2,128,128]{3,2,1,0:T(8,128)(2,1)S(1)}, u32[]{:S(2)}, u32[]{:S(2)}) collective-permute-start(bf16[2,2,128,128]{3,2,1,0:T(8,128)(2,1)S(1)} %get-tuple-element.40), channel_id=1, source_target_pairs={{0,4},{1,5},{2,6},{3,7},{4,0},{5,1},{6,2},{7,3},{8,12},{9,13},{10,... | collective-permute-start | bytes 393224 | tf_op jit(solution)/shard_map/ppermute | solution.py:561
  13.6 6.7 %collective-permute-start.3 = (bf16[2,2,128,128]{3,2,1,0:T(8,128)(2,1)S(1)}, bf16[2,2,128,128]{3,2,1,0:T(8,128)(2,1)S(1)}, u32[]{:S(2)}, u32[]{:S(2)}) collective-permute-start(bf16[2,2,128,128]{3,2,1,0:T(8,128)(2,1)S(1)} %get-tuple-element.41), channel_id=1, source_target_pairs={{0,6},{1,7},{2,0},{3,1},{4,2},{5,3},{6,4},{7,5},{8,14},{9,15},{10,... | collective-permute-start | bytes 393224 | tf_op jit(solution)/shard_map/ppermute | solution.py:561
  20.8 7.7 %collective-permute-start.4 = (bf16[2,128,128]{2,1,0:T(8,128)(2,1)S(1)}, bf16[2,128,128]{2,1,0:T(8,128)(2,1)S(1)}, u32[]{:S(2)}, u32[]{:S(2)}) collective-permute-start(bf16[2,128,128]{2,1,0:T(8,128)(2,1)S(1)} %get-tuple-element.47), channel_id=1, source_target_pairs={{0,8},{1,9},{2,10},{3,11},{4,12},{5,13},{6,14},{7,15},{16,24},{17,... | collective-permute-start | bytes 196616 | tf_op jit(solution)/shard_map/ppermute | solution.py:572
  22.3 11.8 %copy-start = (f32[1,128]{1,0:T(1,128)S(1)}, f32[1,128]{1,0:T(1,128)}, u32[]{:S(2)}) copy-start(f32[1,128]{1,0:T(1,128)} %gain_ref.3) | copy-start | bytes 1540
  28.8 7.8 %collective-permute-start.5 = (bf16[2,128,128]{2,1,0:T(8,128)(2,1)S(1)}, bf16[2,128,128]{2,1,0:T(8,128)(2,1)S(1)}, u32[]{:S(2)}, u32[]{:S(2)}) collective-permute-start(bf16[2,128,128]{2,1,0:T(8,128)(2,1)S(1)} %get-tuple-element.49), channel_id=1, source_target_pairs={{0,2},{1,3},{2,4},{3,5},{4,6},{5,7},{6,0},{7,1},{8,10},{9,11},{10,... | collective-permute-start | bytes 196616 | tf_op jit(solution)/shard_map/ppermute | solution.py:561
  30.2 6.4 %collective-permute-start.6 = (bf16[2,128,128]{2,1,0:T(8,128)(2,1)S(1)}, bf16[2,128,128]{2,1,0:T(8,128)(2,1)S(1)}, u32[]{:S(2)}, u32[]{:S(2)}) collective-permute-start(bf16[2,128,128]{2,1,0:T(8,128)(2,1)S(1)} %get-tuple-element.50), channel_id=1, source_target_pairs={{0,4},{1,5},{2,6},{3,7},{4,0},{5,1},{6,2},{7,3},{8,12},{9,13},{10,... | collective-permute-start | bytes 196616 | tf_op jit(solution)/shard_map/ppermute | solution.py:561
  32.6 4.3 %collective-permute-start.7 = (bf16[2,128,128]{2,1,0:T(8,128)(2,1)S(1)}, bf16[2,128,128]{2,1,0:T(8,128)(2,1)S(1)}, u32[]{:S(2)}, u32[]{:S(2)}) collective-permute-start(bf16[2,128,128]{2,1,0:T(8,128)(2,1)S(1)} %get-tuple-element.51), channel_id=1, source_target_pairs={{0,6},{1,7},{2,0},{3,1},{4,2},{5,3},{6,4},{7,5},{8,14},{9,15},{10,... | collective-permute-start | bytes 196616 | tf_op jit(solution)/shard_map/ppermute | solution.py:561
  34.6 10.9 %collective-permute-start.8 = (bf16[256,256]{1,0:T(8,128)(2,1)S(1)}, bf16[256,256]{1,0:T(8,128)(2,1)S(1)}, u32[]{:S(2)}, u32[]{:S(2)}) collective-permute-start(bf16[256,256]{1,0:T(8,128)(2,1)S(1)} %finish_own.1), channel_id=1, source_target_pairs={{0,16},{16,32},{32,48},{48,64},{64,80},{80,96},{96,112},{112,128},... | collective-permute-start | bytes 393224 | tf_op jit(solution)/shard_map/ppermute | solution.py:586
  37.6 14.5 %collective-permute-start.10 = (bf16[256,768]{1,0:T(8,128)(2,1)S(1)}, bf16[256,768]{1,0:T(8,128)(2,1)S(1)}, u32[]{:S(2)}, u32[]{:S(2)}) collective-permute-start(bf16[256,768]{1,0:T(8,128)(2,1)S(1)} %finish_rest.1), channel_id=1, source_target_pairs={{0,16},{16,32},{32,48},{48,64},{64,80},{80,96},{96,112},{112,128},... | collective-permute-start | bytes 1179656 | tf_op jit(solution)/shard_map/ppermute | solution.py:586
  45.8 1.6 %collective-permute-start.9 = (bf16[8,128,128]{2,1,0:T(8,128)(2,1)S(1)}, bf16[8,128,128]{2,1,0:T(8,128)(2,1)S(1)}, u32[]{:S(2)}, u32[]{:S(2)}) collective-permute-start(bf16[8,128,128]{2,1,0:T(8,128)(2,1)S(1)} %other_core.1), channel_id=1, source_target_pairs={{0,1},{1,0},{2,3},{3,2},{4,5},{5,4},{6,7},{7,6},{8,9},{9,8},{10,11... | collective-permute-start | bytes 786440 | tf_op jit(solution)/shard_map/ppermute | solution.py:553
  47.8 11.3 %collective-permute-start.12 = (bf16[256,512]{1,0:T(8,128)(2,1)S(1)}, bf16[256,512]{1,0:T(8,128)(2,1)S(1)}, u32[]{:S(2)}, u32[]{:S(2)}) collective-permute-start(bf16[256,512]{1,0:T(8,128)(2,1)S(1)} %finish_far.3), channel_id=1, source_target_pairs={{0,16},{16,32},{32,48},{48,64},{64,80},{80,96},{96,112},{112,128},... | collective-permute-start | bytes 786440 | tf_op jit(solution)/shard_map/ppermute | solution.py:586
  52.5 11.5 %collective-permute-start.11 = (bf16[256,512]{1,0:T(8,128)(2,1)S(1)}, bf16[256,512]{1,0:T(8,128)(2,1)S(1)}, u32[]{:S(2)}, u32[]{:S(2)}) collective-permute-start(bf16[256,512]{1,0:T(8,128)(2,1)S(1)} %finish_far.2), channel_id=1, source_target_pairs={{0,16},{16,32},{32,48},{48,64},{64,80},{80,96},{96,112},{112,128},... | collective-permute-start | bytes 786440 | tf_op jit(solution)/shard_map/ppermute | solution.py:586

commit v3 on v2

--- a/solution.py
+++ b/solution.py
@@ -14,6 +14,7 @@
 BASE = 8
 GROUP = 8
 XS = 4
+FAR = 5
 SPLIT = 4
 VMEM = pl.BlockSpec(memory_space=pltpu.VMEM)
 
@@ -529,7 +530,8 @@
 def place_last_kernel(far2, _, out_hbm, sems):
     core, _ = place()
     cols = far2.shape[1]
-    at = pl.multiple_of((1 - core) * 2 * cols + cols, 128)
+    mid = out_hbm.shape[1] // 2
+    at = pl.multiple_of((1 - core) * mid + mid - cols, 128)
     for copy in fetch([(far2, out_hbm.at[:, pl.ds(at, cols)])], sems):
         copy.wait()
 
@@ -612,17 +614,17 @@
     )[0]
     got = swap_cores(theirs)
 
-    def finish_far(first, after):
+    def finish_far(first, count, after):
         done = small_call(
             functools.partial(far_kernel, first),
-            [(tokens, width // 4)],
+            [(tokens, count * 128)],
             (far, got, x, out_gain, after),
             "finish_far",
         )[0]
         return next_section(done)
 
-    done_far1 = finish_far(0, done_own)
-    done_far2 = finish_far(keep.shape[0] // 2, done_rest)
+    done_far1 = finish_far(0, FAR, done_own)
+    done_far2 = finish_far(FAR, keep.shape[0] - FAR, done_rest)
     most = place_columns(width, place_kernel, (done_own, done_rest, done_far1), "place_most")
     return place_columns(width, place_last_kernel, (done_far2,), "place_last", most)[None]
 

time: 65 us -> 67.2 us (1.034)
  starting transfers between devices: 16.9 us -> 18.7 us
    ppermute x6, waiting for transfers between devices: 4.17 us -> 6.63 us  [along_x(): return lax.ppermute(array, 'ctx', pairs)]
    ppermute x4, starting transfers between devices: 4.14 us -> 6.06 us  [next_section(): return lax.ppermute(array, 'section', [(i, (i + 1) % n) for i in range(n)])]
    ppermute x2, waiting for transfers between devices: 1.52 us -> 0.01 us  [swap_cores(): lax.ppermute(array, 'ctx', [(i, i ^ 1) for i in range(lax.axis_size('ctx'...]
  transfers between devices with their start and end apart: 13 -> 13, of which waited for: 9 -> 9; matrix products, arithmetic and copies ran while one was open for 0% -> 0% of each run, Pallas kernels for 15% -> 13%
where the time goes in v3:
time: 67.2 us; the launch traced here: 67 us
  waiting for transfers between devices  31 us (46%)
  starting transfers between devices  18.7 us (28%)
  Pallas kernels  16.9 us (25%)
    ppermute x4, waiting for transfers between devices, next_section(): return lax.ppermute(array, 'section', [(i, (i + 1) % n) for i in range(n)])  20 us
    ppermute x6, starting transfers between devices, along_x(): return lax.ppermute(array, 'ctx', pairs)  11 us
    pallas_call x2, Pallas kernels, pairs_call(): pl.pallas_call(kernel, in_specs=in_specs, out_specs=[VMEM] * len(outs), o...  8.81 us
    ppermute x6, waiting for transfers between devices, along_x(): return lax.ppermute(array, 'ctx', pairs)  6.63 us
    pallas_call x11, Pallas kernels, small_call(): pl.pallas_call(kernel, in_specs=[VMEM] * len(args), out_specs=[VMEM] * le...  6.48 us
    ppermute x4, starting transfers between devices, next_section(): return lax.ppermute(array, 'section', [(i, (i + 1) % n) for i in range(n)])  6.06 us
    ppermute x1, waiting for transfers between devices, row_starts(): before = lax.ppermute(total, 'ctx', [(i, i + row) for i in range(row)])  4.39 us
    pallas_call x2, Pallas kernels, place_columns(): pl.pallas_call(kernel, in_specs=[VMEM] * len(parts) + [hbm] * len(last),...  1.66 us
  transfers between devices with their start and end apart: 13, of which 9 were waited for; matrix products, arithmetic and copies ran while one was open for 0% of the time, Pallas kernels for 13%

profile of v3, /device:TPU:16, one launch (start us, length us, event | category | flops | bytes accessed | tf_op | source)
XLA Modules:
  0.0 67.0 jit_solution(4231868405061903334)
XLA Ops:
  0.0 5.5 %first_pairs.1 = (bf16[8,2,128,128]{3,2,1,0:T(8,128)(2,1)S(1)}, bf16[256,512]{1,0:T(8,128)(2,1)S(1)}, bf16[8,256,256]{2,1,0:T(8,128)(2,1)S(1)}, bf16[256,2048]{1...) custom-call(bf16[256,2048]{1,0:T(8,128)(2,1)} %bitcast.6, ...), custom_call_target="tpu_custom_call" | custom-call | flops 5000000000 | bytes 8000000 | tf_op jit(solution)/shard_map/first_pairs/pallas_call | solution.py:262
  5.5 0.1 collective-permute-start
  5.6 3.3 %last_pairs.1 = (bf16[8,2,128,128]{3,2,1,0:T(8,128)(2,1)S(1)}, bf16[256,512]{1,0:T(8,128)(2,1)S(1)}, bf16[8,256,256]{2,1,0:T(8,128)(2,1)S(1)}) custom-call(bf16[256,2048]{1,0:T(8,128)(2,1)S(1)} %get-tuple-element.29.normed, bf16[2,2048,512]{2,1,0:T(8,128)(2,1)S(1)} %get-tuple-element.35.wk, f32[16,256]{1,0:T(8,128)S(1)} %get-tuple-element.33.cumul_ref, ...), custom_call_target="tpu_custom_call" | custom-call | flops 5000000000 | bytes 8000000 | tf_op jit(solution)/shard_map/last_pairs/pallas_call | solution.py:262
  8.9 0.0 collective-permute-done.other.refs_1_.refs_5_.refs_4_
  8.9 0.3 compose.1
  9.3 1.6 %collective-permute-start.1 = (bf16[2,2,128,128]{3,2,1,0:T(8,128)(2,1)S(1)}, bf16[2,2,128,128]{3,2,1,0:T(8,128)(2,1)S(1)}, u32[]{:S(2)}, u32[]{:S(2)}) collective-permute-start(bf16[2,2,128,128]{3,2,1,0:T(8,128)(2,1)S(1)} %get-tuple-element.39), channel_id=1, source_target_pairs={{0,2},{1,3},{2,4},{3,5},{4,6},{5,7},{6,0},{7,1},{8,10},{9,11},{10,... | collective-permute-start | bytes 393224 | tf_op jit(solution)/shard_map/ppermute | solution.py:563
  10.8 2.7 %collective-permute-start.2 = (bf16[2,2,128,128]{3,2,1,0:T(8,128)(2,1)S(1)}, bf16[2,2,128,128]{3,2,1,0:T(8,128)(2,1)S(1)}, u32[]{:S(2)}, u32[]{:S(2)}) collective-permute-start(bf16[2,2,128,128]{3,2,1,0:T(8,128)(2,1)S(1)} %get-tuple-element.40), channel_id=1, source_target_pairs={{0,4},{1,5},{2,6},{3,7},{4,0},{5,1},{6,2},{7,3},{8,12},{9,13},{10,... | collective-permute-start | bytes 393224 | tf_op jit(solution)/shard_map/ppermute | solution.py:563
  13.6 1.4 %collective-permute-start.3 = (bf16[2,2,128,128]{3,2,1,0:T(8,128)(2,1)S(1)}, bf16[2,2,128,128]{3,2,1,0:T(8,128)(2,1)S(1)}, u32[]{:S(2)}, u32[]{:S(2)}) collective-permute-start(bf16[2,2,128,128]{3,2,1,0:T(8,128)(2,1)S(1)} %get-tuple-element.41), channel_id=1, source_target_pairs={{0,6},{1,7},{2,0},{3,1},{4,2},{5,3},{6,4},{7,5},{8,14},{9,15},{10,... | collective-permute-start | bytes 393224 | tf_op jit(solution)/shard_map/ppermute | solution.py:563
  15.0 1.3 %local_rows.3.refs_4_.refs_2_.refs_5_ = bf16[2,256,1024]{2,1,0:T(8,128)(2,1)S(1)} custom-call(bf16[256,2048]{1,0:T(8,128)(2,1)S(1)} %get-tuple-element.29.normed, bf16[2,2048,512]{2,1,0:T(8,128)(2,1)S(1)} %get-tuple-element.30.wq, bf16[256,512]{1,0:T(8,128)(2,1)S(1)} %get-tuple-element.42.unit_keys, bf16[8,256,256]{2,1,0:T(8,128)(2,1)S(1)} %get-tuple-element.43.solved_ref, ...), custom_call_target="tpu_custom_call" | custom-call | tf_op jit(solution)/shard_map/local_rows/pallas_call | solution.py:357
  16.3 0.1 collective-permute-done.1.refs_1_
  16.5 3.8 %collective-permute-done.2.refs_2_ = bf16[2,2,128,128]{3,2,1,0:T(8,128)(2,1)S(1)} collective-permute-done((bf16[2,2,128,128]{3,2,1,0:T(8,128)(2,1)S(1)}, bf16[2,2,128,128]{3,2,1,0:T(8,128)(2,1)S(1)}, u32[]{:S(2)}, u32[]{:S(2)}) %collective-permute-start.2) | collective-permute-done | bytes 131104 | tf_op jit(solution)/shard_map/ppermute | solution.py:563
  20.2 0.0 collective-permute-done.3.refs_3_
  20.2 0.6 row_total.1
  20.8 1.5 %collective-permute-start.4 = (bf16[2,128,128]{2,1,0:T(8,128)(2,1)S(1)}, bf16[2,128,128]{2,1,0:T(8,128)(2,1)S(1)}, u32[]{:S(2)}, u32[]{:S(2)}) collective-permute-start(bf16[2,128,128]{2,1,0:T(8,128)(2,1)S(1)} %get-tuple-element.47), channel_id=1, source_target_pairs={{0,8},{1,9},{2,10},{3,11},{4,12},{5,13},{6,14},{7,15},{16,24},{17,... | collective-permute-start | bytes 196616 | tf_op jit(solution)/shard_map/ppermute | solution.py:574
  22.3 0.0 copy-start
  22.3 1.3 %local_rows.2._.far = bf16[2,256,1024]{2,1,0:T(8,128)(2,1)S(1)} custom-call(bf16[256,2048]{1,0:T(8,128)(2,1)S(1)} %get-tuple-element.29.normed, bf16[2,2048,512]{2,1,0:T(8,128)(2,1)S(1)} %get-tuple-element.30.wq, bf16[256,512]{1,0:T(8,128)(2,1)S(1)} %get-tuple-element.31.unit_keys, bf16[8,256,256]{2,1,0:T(8,128)(2,1)S(1)} %get-tuple-element.32.solved_ref, ...), custom_call_target="tpu_custom_call" | custom-call | tf_op jit(solution)/shard_map/local_rows/pallas_call | solution.py:357
  23.6 0.4 row_pairs.1
  24.1 4.4 %collective-permute-done.4.before = bf16[2,128,128]{2,1,0:T(8,128)(2,1)S(1)} collective-permute-done((bf16[2,128,128]{2,1,0:T(8,128)(2,1)S(1)}, bf16[2,128,128]{2,1,0:T(8,128)(2,1)S(1)}, u32[]{:S(2)}, u32[]{:S(2)}) %collective-permute-start.4) | collective-permute-done | bytes 65568 | tf_op jit(solution)/shard_map/ppermute | solution.py:574
  28.5 0.3 row_starts.1
  28.8 0.0 copy-done
  28.8 0.5 finish_own.1
  29.2 2.0 %collective-permute-start.8 = (bf16[256,256]{1,0:T(8,128)(2,1)S(1)}, bf16[256,256]{1,0:T(8,128)(2,1)S(1)}, u32[]{:S(2)}, u32[]{:S(2)}) collective-permute-start(bf16[256,256]{1,0:T(8,128)(2,1)S(1)} %finish_own.1), channel_id=1, source_target_pairs={{0,16},{16,32},{32,48},{48,64},{64,80},{80,96},{96,112},{112,128},... | collective-permute-start | bytes 393224 | tf_op jit(solution)/shard_map/ppermute | solution.py:588
  31.2 1.3 %collective-permute-start.5 = (bf16[2,128,128]{2,1,0:T(8,128)(2,1)S(1)}, bf16[2,128,128]{2,1,0:T(8,128)(2,1)S(1)}, u32[]{:S(2)}, u32[]{:S(2)}) collective-permute-start(bf16[2,128,128]{2,1,0:T(8,128)(2,1)S(1)} %get-tuple-element.49), channel_id=1, source_target_pairs={{0,2},{1,3},{2,4},{3,5},{4,6},{5,7},{6,0},{7,1},{8,10},{9,11},{10,... | collective-permute-start | bytes 196616 | tf_op jit(solution)/shard_map/ppermute | solution.py:563
  32.6 2.4 %collective-permute-start.6 = (bf16[2,128,128]{2,1,0:T(8,128)(2,1)S(1)}, bf16[2,128,128]{2,1,0:T(8,128)(2,1)S(1)}, u32[]{:S(2)}, u32[]{:S(2)}) collective-permute-start(bf16[2,128,128]{2,1,0:T(8,128)(2,1)S(1)} %get-tuple-element.50), channel_id=1, source_target_pairs={{0,4},{1,5},{2,6},{3,7},{4,0},{5,1},{6,2},{7,3},{8,12},{9,13},{10,... | collective-permute-start | bytes 196616 | tf_op jit(solution)/shard_map/ppermute | solution.py:563
  35.0 1.6 %collective-permute-start.7 = (bf16[2,128,128]{2,1,0:T(8,128)(2,1)S(1)}, bf16[2,128,128]{2,1,0:T(8,128)(2,1)S(1)}, u32[]{:S(2)}, u32[]{:S(2)}) collective-permute-start(bf16[2,128,128]{2,1,0:T(8,128)(2,1)S(1)} %get-tuple-element.51), channel_id=1, source_target_pairs={{0,6},{1,7},{2,0},{3,1},{4,2},{5,3},{6,4},{7,5},{8,14},{9,15},{10,... | collective-permute-start | bytes 196616 | tf_op jit(solution)/shard_map/ppermute | solution.py:563
  36.5 0.2 collective-permute-done.5.refs_1_.refs_0_
  36.7 1.6 %collective-permute-done.6.refs_2_.refs_1_ = bf16[2,128,128]{2,1,0:T(8,128)(2,1)S(1)} collective-permute-done((bf16[2,128,128]{2,1,0:T(8,128)(2,1)S(1)}, bf16[2,128,128]{2,1,0:T(8,128)(2,1)S(1)}, u32[]{:S(2)}, u32[]{:S(2)}) %collective-permute-start.6) | collective-permute-done | bytes 65568 | tf_op jit(solution)/shard_map/ppermute | solution.py:563
  38.3 0.9 %collective-permute-done.7.refs_3_.refs_2_ = bf16[2,128,128]{2,1,0:T(8,128)(2,1)S(1)} collective-permute-done((bf16[2,128,128]{2,1,0:T(8,128)(2,1)S(1)}, bf16[2,128,128]{2,1,0:T(8,128)(2,1)S(1)}, u32[]{:S(2)}, u32[]{:S(2)}) %collective-permute-start.7) | collective-permute-done | bytes 65568 | tf_op jit(solution)/shard_map/ppermute | solution.py:563
  39.2 0.0 collective-permute-done.8.refs_6_._.own
  39.2 0.2 other_core.1
  39.5 0.1 collective-permute-start.9
  39.6 0.7 %finish_rest.1 = bf16[256,768]{1,0:T(8,128)(2,1)S(1)} custom-call(bf16[2,128,128]{2,1,0:T(8,128)(2,1)S(1)} %collective-permute-done.5.refs_1_.refs_0_, bf16[2,128,128]{2,1,0:T(8,128)(2,1)S(1)} %collective-permute-done.6.refs_2_.refs_1_, bf16[2,128,128]{2,1,0:T(8,128)(2,1)S(1)} %collective-permute-done.7.refs_3_.refs_2_, ...), custom_call_target="tpu_custom_call" | custom-call | tf_op jit(solution)/shard_map/finish_rest/pallas_call | solution.py:357
  40.3 2.0 %collective-permute-start.10 = (bf16[256,768]{1,0:T(8,128)(2,1)S(1)}, bf16[256,768]{1,0:T(8,128)(2,1)S(1)}, u32[]{:S(2)}, u32[]{:S(2)}) collective-permute-start(bf16[256,768]{1,0:T(8,128)(2,1)S(1)} %finish_rest.1), channel_id=1, source_target_pairs={{0,16},{16,32},{32,48},{48,64},{64,80},{80,96},{96,112},{112,128},... | collective-permute-start | bytes 1179656 | tf_op jit(solution)/shard_map/ppermute | solution.py:588
  42.3 0.0 collective-permute-done.9.got
  42.3 0.5 finish_far.3
  42.8 2.0 %collective-permute-start.12 = (bf16[256,640]{1,0:T(8,128)(2,1)S(1)}, bf16[256,640]{1,0:T(8,128)(2,1)S(1)}, u32[]{:S(2)}, u32[]{:S(2)}) collective-permute-start(bf16[256,640]{1,0:T(8,128)(2,1)S(1)} %finish_far.3), channel_id=1, source_target_pairs={{0,16},{16,32},{32,48},{48,64},{64,80},{80,96},{96,112},{112,128},... | collective-permute-start | bytes 983048 | tf_op jit(solution)/shard_map/ppermute | solution.py:588
  44.8 10.3 %collective-permute-done.10._.rest = bf16[256,768]{1,0:T(8,128)(2,1)S(1)} collective-permute-done((bf16[256,768]{1,0:T(8,128)(2,1)S(1)}, bf16[256,768]{1,0:T(8,128)(2,1)S(1)}, u32[]{:S(2)}, u32[]{:S(2)}) %collective-permute-start.10) | collective-permute-done | bytes 393248 | tf_op jit(solution)/shard_map/ppermute | solution.py:588
  55.1 0.4 finish_far.2
  55.5 0.1 collective-permute-start.11
  55.6 6.6 %collective-permute-done.12.far1 = bf16[256,640]{1,0:T(8,128)(2,1)S(1)} collective-permute-done((bf16[256,640]{1,0:T(8,128)(2,1)S(1)}, bf16[256,640]{1,0:T(8,128)(2,1)S(1)}, u32[]{:S(2)}, u32[]{:S(2)}) %collective-permute-start.12) | collective-permute-done | bytes 327712 | tf_op jit(solution)/shard_map/ppermute | solution.py:588
  62.1 0.9 %place_most.1._ = bf16[256,2048]{1,0:T(8,128)(2,1)} custom-call(bf16[256,256]{1,0:T(8,128)(2,1)S(1)} %collective-permute-done.8.refs_6_._.own, bf16[256,768]{1,0:T(8,128)(2,1)S(1)} %collective-permute-done.10._.rest, bf16[256,640]{1,0:T(8,128)(2,1)S(1)} %collective-permute-done.12.far1), custom_call_target="tpu_custom_call" | custom-call | tf_op jit(solution)/shard_map/place_most/pallas_call | solution.py:542
  63.1 3.1 %collective-permute-done.11.far2 = bf16[256,384]{1,0:T(8,128)(2,1)S(1)} collective-permute-done((bf16[256,384]{1,0:T(8,128)(2,1)S(1)}, bf16[256,384]{1,0:T(8,128)(2,1)S(1)}, u32[]{:S(2)}, u32[]{:S(2)}) %collective-permute-start.11) | collective-permute-done | bytes 196640 | tf_op jit(solution)/shard_map/ppermute | solution.py:588
  66.1 0.7 %place_last.1 = bf16[256,2048]{1,0:T(8,128)(2,1)} custom-call(bf16[256,384]{1,0:T(8,128)(2,1)S(1)} %collective-permute-done.11.far2, bf16[256,2048]{1,0:T(8,128)(2,1)} %place_most.1._), custom_call_target="tpu_custom_call", output_to_operand_aliasing={{}: (1, {})} | custom-call | tf_op jit(solution)/shard_map/place_last/pallas_call | solution.py:542
Async XLA Ops:
  5.5 3.4 %collective-permute-start = (bf16[8,2,128,128]{3,2,1,0:T(8,128)(2,1)S(1)}, bf16[8,2,128,128]{3,2,1,0:T(8,128)(2,1)S(1)}, u32[]{:S(2)}, u32[]{:S(2)}) collective-permute-start(bf16[8,2,128,128]{3,2,1,0:T(8,128)(2,1)S(1)} %get-tuple-element.37), channel_id=1, source_target_pairs={{0,1},{1,0},{2,3},{3,2},{4,5},{5,4},{6,7},{7,6},{8,9},{9,8},{10,11... | collective-permute-start | bytes 1572872 | tf_op jit(solution)/shard_map/ppermute | solution.py:555
  9.3 7.2 %collective-permute-start.1 = (bf16[2,2,128,128]{3,2,1,0:T(8,128)(2,1)S(1)}, bf16[2,2,128,128]{3,2,1,0:T(8,128)(2,1)S(1)}, u32[]{:S(2)}, u32[]{:S(2)}) collective-permute-start(bf16[2,2,128,128]{3,2,1,0:T(8,128)(2,1)S(1)} %get-tuple-element.39), channel_id=1, source_target_pairs={{0,2},{1,3},{2,4},{3,5},{4,6},{5,7},{6,0},{7,1},{8,10},{9,11},{10,... | collective-permute-start | bytes 393224 | tf_op jit(solution)/shard_map/ppermute | solution.py:563
  10.8 9.4 %collective-permute-start.2 = (bf16[2,2,128,128]{3,2,1,0:T(8,128)(2,1)S(1)}, bf16[2,2,128,128]{3,2,1,0:T(8,128)(2,1)S(1)}, u32[]{:S(2)}, u32[]{:S(2)}) collective-permute-start(bf16[2,2,128,128]{3,2,1,0:T(8,128)(2,1)S(1)} %get-tuple-element.40), channel_id=1, source_target_pairs={{0,4},{1,5},{2,6},{3,7},{4,0},{5,1},{6,2},{7,3},{8,12},{9,13},{10,... | collective-permute-start | bytes 393224 | tf_op jit(solution)/shard_map/ppermute | solution.py:563
  13.6 6.7 %collective-permute-start.3 = (bf16[2,2,128,128]{3,2,1,0:T(8,128)(2,1)S(1)}, bf16[2,2,128,128]{3,2,1,0:T(8,128)(2,1)S(1)}, u32[]{:S(2)}, u32[]{:S(2)}) collective-permute-start(bf16[2,2,128,128]{3,2,1,0:T(8,128)(2,1)S(1)} %get-tuple-element.41), channel_id=1, source_target_pairs={{0,6},{1,7},{2,0},{3,1},{4,2},{5,3},{6,4},{7,5},{8,14},{9,15},{10,... | collective-permute-start | bytes 393224 | tf_op jit(solution)/shard_map/ppermute | solution.py:563
  20.8 7.7 %collective-permute-start.4 = (bf16[2,128,128]{2,1,0:T(8,128)(2,1)S(1)}, bf16[2,128,128]{2,1,0:T(8,128)(2,1)S(1)}, u32[]{:S(2)}, u32[]{:S(2)}) collective-permute-start(bf16[2,128,128]{2,1,0:T(8,128)(2,1)S(1)} %get-tuple-element.47), channel_id=1, source_target_pairs={{0,8},{1,9},{2,10},{3,11},{4,12},{5,13},{6,14},{7,15},{16,24},{17,... | collective-permute-start | bytes 196616 | tf_op jit(solution)/shard_map/ppermute | solution.py:574
  22.3 6.5 %copy-start = (f32[1,128]{1,0:T(1,128)S(1)}, f32[1,128]{1,0:T(1,128)}, u32[]{:S(2)}) copy-start(f32[1,128]{1,0:T(1,128)} %gain_ref.3) | copy-start | bytes 1540
  29.2 10.0 %collective-permute-start.8 = (bf16[256,256]{1,0:T(8,128)(2,1)S(1)}, bf16[256,256]{1,0:T(8,128)(2,1)S(1)}, u32[]{:S(2)}, u32[]{:S(2)}) collective-permute-start(bf16[256,256]{1,0:T(8,128)(2,1)S(1)} %finish_own.1), channel_id=1, source_target_pairs={{0,16},{16,32},{32,48},{48,64},{64,80},{80,96},{96,112},{112,128},... | collective-permute-start | bytes 393224 | tf_op jit(solution)/shard_map/ppermute | solution.py:588
  31.2 5.5 %collective-permute-start.5 = (bf16[2,128,128]{2,1,0:T(8,128)(2,1)S(1)}, bf16[2,128,128]{2,1,0:T(8,128)(2,1)S(1)}, u32[]{:S(2)}, u32[]{:S(2)}) collective-permute-start(bf16[2,128,128]{2,1,0:T(8,128)(2,1)S(1)} %get-tuple-element.49), channel_id=1, source_target_pairs={{0,2},{1,3},{2,4},{3,5},{4,6},{5,7},{6,0},{7,1},{8,10},{9,11},{10,... | collective-permute-start | bytes 196616 | tf_op jit(solution)/shard_map/ppermute | solution.py:563
  32.6 5.8 %collective-permute-start.6 = (bf16[2,128,128]{2,1,0:T(8,128)(2,1)S(1)}, bf16[2,128,128]{2,1,0:T(8,128)(2,1)S(1)}, u32[]{:S(2)}, u32[]{:S(2)}) collective-permute-start(bf16[2,128,128]{2,1,0:T(8,128)(2,1)S(1)} %get-tuple-element.50), channel_id=1, source_target_pairs={{0,4},{1,5},{2,6},{3,7},{4,0},{5,1},{6,2},{7,3},{8,12},{9,13},{10,... | collective-permute-start | bytes 196616 | tf_op jit(solution)/shard_map/ppermute | solution.py:563
  35.0 4.3 %collective-permute-start.7 = (bf16[2,128,128]{2,1,0:T(8,128)(2,1)S(1)}, bf16[2,128,128]{2,1,0:T(8,128)(2,1)S(1)}, u32[]{:S(2)}, u32[]{:S(2)}) collective-permute-start(bf16[2,128,128]{2,1,0:T(8,128)(2,1)S(1)} %get-tuple-element.51), channel_id=1, source_target_pairs={{0,6},{1,7},{2,0},{3,1},{4,2},{5,3},{6,4},{7,5},{8,14},{9,15},{10,... | collective-permute-start | bytes 196616 | tf_op jit(solution)/shard_map/ppermute | solution.py:563
  39.5 2.8 %collective-permute-start.9 = (bf16[8,128,128]{2,1,0:T(8,128)(2,1)S(1)}, bf16[8,128,128]{2,1,0:T(8,128)(2,1)S(1)}, u32[]{:S(2)}, u32[]{:S(2)}) collective-permute-start(bf16[8,128,128]{2,1,0:T(8,128)(2,1)S(1)} %other_core.1), channel_id=1, source_target_pairs={{0,1},{1,0},{2,3},{3,2},{4,5},{5,4},{6,7},{7,6},{8,9},{9,8},{10,11... | collective-permute-start | bytes 786440 | tf_op jit(solution)/shard_map/ppermute | solution.py:555
  40.3 14.8 %collective-permute-start.10 = (bf16[256,768]{1,0:T(8,128)(2,1)S(1)}, bf16[256,768]{1,0:T(8,128)(2,1)S(1)}, u32[]{:S(2)}, u32[]{:S(2)}) collective-permute-start(bf16[256,768]{1,0:T(8,128)(2,1)S(1)} %finish_rest.1), channel_id=1, source_target_pairs={{0,16},{16,32},{32,48},{48,64},{64,80},{80,96},{96,112},{112,128},... | collective-permute-start | bytes 1179656 | tf_op jit(solution)/shard_map/ppermute | solution.py:588
  42.8 19.3 %collective-permute-start.12 = (bf16[256,640]{1,0:T(8,128)(2,1)S(1)}, bf16[256,640]{1,0:T(8,128)(2,1)S(1)}, u32[]{:S(2)}, u32[]{:S(2)}) collective-permute-start(bf16[256,640]{1,0:T(8,128)(2,1)S(1)} %finish_far.3), channel_id=1, source_target_pairs={{0,16},{16,32},{32,48},{48,64},{64,80},{80,96},{96,112},{112,128},... | collective-permute-start | bytes 983048 | tf_op jit(solution)/shard_map/ppermute | solution.py:588
  55.5 10.7 %collective-permute-start.11 = (bf16[256,384]{1,0:T(8,128)(2,1)S(1)}, bf16[256,384]{1,0:T(8,128)(2,1)S(1)}, u32[]{:S(2)}, u32[]{:S(2)}) collective-permute-start(bf16[256,384]{1,0:T(8,128)(2,1)S(1)} %finish_far.2), channel_id=1, source_target_pairs={{0,16},{16,32},{32,48},{48,64},{64,80},{80,96},{96,112},{112,128},... | collective-permute-start | bytes 589832 | tf_op jit(solution)/shard_map/ppermute | solution.py:588
